TPU v7x, 32 devices: a whole 2x2x4 slice. The times are simulated.
32 devices in a mesh: dp: 2 (over x), row: 4 (over y, core), col: 4 (over z).
Axes of the slice: x: 2, y: 2, z: 4, core: 2. Of those that a mesh axis runs over, the one named last changes fastest.
Arguments:
- layer_input: bfloat16 [32768, 1024], P(('dp', 'col'), 'row'), may hold values from -6 to 6
- gain_one: float32 [1024], P('row'), may hold values from 0.5 to 1.5
- gain_two: float32 [1024], P('row'), may hold values from 0.5 to 1.5
- query_key_value_weight: bfloat16 [1024, 3, 1024], P('row', None, 'col'), may hold values from -0.1875 to 0.1875
- w_out: bfloat16 [1024, 1024], P('col', 'row'), may hold values from -3.5 to 3.5
- w_in: bfloat16 [1024, 2, 2624], P('row', None, 'col'), may hold values from -0.1875 to 0.1875
- w_down: bfloat16 [2624, 1024], P('col', 'row'), may hold values from -0.125 to 0.125
- cotangent: bfloat16 [32768, 1024], P(('dp', 'col'), 'row'), may hold values from -6 to 6
Outputs:
- output: bfloat16 [32768, 1024], P(('dp', 'col'), 'row')
- grad_input: bfloat16 [32768, 1024], P(('dp', 'col'), 'row')
- grad_w_qkv: float32 [1024, 3, 1024], P('row', None, 'col')
- grad_w_out: float32 [1024, 1024], P('col', 'row')
- grad_w_in: float32 [1024, 2, 2624], P('row', None, 'col')
- grad_w_down: float32 [2624, 1024], P('col', 'row')
- grad_gain_one: float32 [1024], P('row')
- grad_gain_two: float32 [1024], P('row')
All inputs are finite; a program needn't handle non-finite values.
Results may differ from a plain program's by a relative error of at most 0.015.
Values may be sent and summed in bfloat16 or wider, within the bound.
A program may use at most 384 MiB of HBM per device.

v0:
```python
import math

import jax
import jax.numpy as jnp
from jax import lax
from jax.sharding import PartitionSpec as P

HD = 64
LEN = 1024


EPSILON = 1e-05
THETA = 160000.0


def turning(rows, size):
    positions = (jnp.arange(rows) % LEN).astype(jnp.float32)
    inverse = THETA ** (-jnp.arange(0, size, 2, dtype=jnp.float32) / size)
    phase = positions[:, None] * inverse[None, :]
    phase = jnp.concatenate([phase, phase], axis=-1)[:, None, :]
    return (jnp.cos(phase), jnp.sin(phase))


def rotate(values, cosine, sine):
    half = values.shape[-1] // 2
    turned = jnp.concatenate([-values[..., half:], values[..., :half]], axis=-1)
    return values * cosine + turned * sine


def unrotate(grads, cosine, sine):
    half = grads.shape[-1] // 2
    moved = grads * sine
    return grads * cosine + jnp.concatenate([moved[..., half:], -moved[..., :half]], axis=-1)


def gating(gate_up_output):
    return jax.nn.gelu(gate_up_output[:, 0], approximate=False) * gate_up_output[:, 1]


def row_totals(pair):
    return lax.psum((pair[0], pair[1]), "row")


def norm_forward(values):
    width = values.shape[1]
    total = jnp.sum(values, axis=1)
    square = jnp.sum(values * values, axis=1)
    width = width * lax.axis_size("row")
    total, square = row_totals((total, square))
    mean = total / width
    rstd = lax.rsqrt(square / width - mean * mean + EPSILON)
    return ((values - mean[:, None]) * rstd[:, None], rstd)


def norm_backward(grads, centred, rstd, gain):
    width = grads.shape[1]
    scaled = grads * gain
    first = jnp.sum(scaled, axis=1)
    second = jnp.sum(scaled * centred, axis=1)
    width = width * lax.axis_size("row")
    first, second = row_totals((first, second))
    result = rstd[:, None] * (scaled - first[:, None] / width - centred * (second[:, None] / width))
    return (result, jnp.sum(grads * centred, axis=0))


def widen_col(values):
    return lax.all_gather(values, "col", axis=0, tiled=True)


def widen_row(values):
    return lax.all_gather(values, "row", axis=0, tiled=True)


def project_row(gathered, weight):
    rows = gathered.shape[0] // lax.axis_size("row")

    def term(start, count):
        return jnp.dot(gathered, weight, preferred_element_type=jnp.float32)

    return lax.psum_scatter(
        term(jnp.int32(0), rows * lax.axis_size("row")), "row", scatter_dimension=0, tiled=True
    )


def project_col(gathered, weight):
    rows = gathered.shape[0] // lax.axis_size("col")

    def term(start, count):
        return jnp.dot(gathered, weight, preferred_element_type=jnp.float32)

    return lax.psum_scatter(
        term(jnp.int32(0), rows * lax.axis_size("col")), "col", scatter_dimension=0, tiled=True
    )


def return_row(gathered, weight):
    rows = gathered.shape[0] // lax.axis_size("row")

    def term(start, count):
        return lax.dot_general(
            gathered, weight, (((1,), (1,)), ((), ())), preferred_element_type=jnp.float32
        )

    return lax.psum_scatter(
        term(jnp.int32(0), rows * lax.axis_size("row")), "row", scatter_dimension=0, tiled=True
    )


def return_col(gathered, weight):
    rows = gathered.shape[0] // lax.axis_size("col")

    def term(start, count):
        return lax.dot_general(
            gathered, weight, (((1,), (1,)), ((), ())), preferred_element_type=jnp.float32
        )

    return lax.psum_scatter(
        term(jnp.int32(0), rows * lax.axis_size("col")), "col", scatter_dimension=0, tiled=True
    )


def weight_grad(inputs, grads):
    return lax.dot_general(
        inputs, grads, (((0,), (0,)), ((), ())), preferred_element_type=jnp.float32
    )


def sum_data(members):
    return (
        lax.psum(members[0].astype(jnp.bfloat16), "dp").astype(jnp.float32),
        lax.psum(members[1].astype(jnp.bfloat16), "dp").astype(jnp.float32),
        lax.psum(members[2].astype(jnp.bfloat16), "dp").astype(jnp.float32),
        lax.psum(members[3].astype(jnp.bfloat16), "dp").astype(jnp.float32),
        lax.psum(members[4].astype(jnp.bfloat16), "dp").astype(jnp.float32),
        lax.psum(members[5].astype(jnp.bfloat16), "dp").astype(jnp.float32),
    )


def attend_forward(query, key, value):
    rows, heads, size = query.shape
    block = math.gcd(LEN, 512)
    scale = size ** (-0.5)

    def one_block(index):
        start = index * block
        first = start // LEN * LEN
        query_block = lax.dynamic_slice_in_dim(query, start, block, 0)
        key_seq = lax.dynamic_slice_in_dim(key, first, LEN, 0)
        value_seq = lax.dynamic_slice_in_dim(value, first, LEN, 0)
        scores = (
            jnp.einsum("qhd,khd->hqk", query_block, key_seq, preferred_element_type=jnp.float32)
            * scale
        )
        top = jnp.max(scores, axis=-1, keepdims=True)
        exponent = jnp.exp(scores - top)
        total = jnp.sum(exponent, axis=-1, keepdims=True)
        probs = (exponent / total).astype(jnp.bfloat16)
        result = jnp.einsum("hqk,khd->qhd", probs, value_seq, preferred_element_type=jnp.float32)
        return (result, (top + jnp.log(total))[..., 0])

    results, log_sums = lax.map(one_block, jnp.arange(rows // block))
    return (results.reshape(rows, heads, size), log_sums)


def attend_backward(query, key, value, log_sums, grad_mixed):
    rows, heads, size = query.shape
    block = math.gcd(LEN, 512)
    scale = size ** (-0.5)

    def one_block(carry, item):
        grad_key, grad_value = carry
        index, log_sum = item
        start = index * block
        first = start // LEN * LEN
        query_block = lax.dynamic_slice_in_dim(query, start, block, 0)
        grad_block = lax.dynamic_slice_in_dim(grad_mixed, start, block, 0)
        key_seq = lax.dynamic_slice_in_dim(key, first, LEN, 0)
        value_seq = lax.dynamic_slice_in_dim(value, first, LEN, 0)
        scores = (
            jnp.einsum("qhd,khd->hqk", query_block, key_seq, preferred_element_type=jnp.float32)
            * scale
        )
        probs = jnp.exp(scores - log_sum[:, :, None])
        value_part = jnp.einsum(
            "hqk,qhd->khd",
            probs.astype(jnp.bfloat16),
            grad_block,
            preferred_element_type=jnp.float32,
        )
        grad_probs = jnp.einsum(
            "qhd,khd->hqk", grad_block, value_seq, preferred_element_type=jnp.float32
        )
        inner = jnp.sum(probs * grad_probs, axis=-1, keepdims=True)
        grad_scores = (probs * (grad_probs - inner)).astype(jnp.bfloat16)
        query_part = (
            jnp.einsum("hqk,khd->qhd", grad_scores, key_seq, preferred_element_type=jnp.float32)
            * scale
        )
        key_part = (
            jnp.einsum("hqk,qhd->khd", grad_scores, query_block, preferred_element_type=jnp.float32)
            * scale
        )
        grad_key = lax.dynamic_update_slice_in_dim(
            grad_key, lax.dynamic_slice_in_dim(grad_key, first, LEN, 0) + key_part, first, 0
        )
        grad_value = lax.dynamic_update_slice_in_dim(
            grad_value, lax.dynamic_slice_in_dim(grad_value, first, LEN, 0) + value_part, first, 0
        )
        return ((grad_key, grad_value), query_part)

    empty = jnp.zeros((rows, heads, size), jnp.float32)
    (grad_key, grad_value), grad_query = lax.scan(
        one_block, (empty, empty), (jnp.arange(rows // block), log_sums)
    )
    return (grad_query.reshape(rows, heads, size), grad_key, grad_value)


def attention_part(attention_projected, rows, heads_here):
    attention_projected = attention_projected.reshape(rows, 3, heads_here, HD)
    cosine, sine = turning(rows, HD)
    query = rotate(attention_projected[:, 0], cosine, sine).astype(jnp.bfloat16)
    key_rot = rotate(attention_projected[:, 1], cosine, sine).astype(jnp.bfloat16)
    value = attention_projected[:, 2].astype(jnp.bfloat16)
    mixed, log_sums = attend_forward(query, key_rot, value)
    return (
        mixed.reshape(rows, -1).astype(jnp.bfloat16),
        (query, key_rot, value, log_sums, cosine, sine),
    )


def attention_back(grad_mixed, kept, rows, heads_here):
    query, key_rot, value, log_sums, cosine, sine = kept
    grad_mixed = grad_mixed.reshape(rows, heads_here, HD)
    grad_query, grad_key, grad_value = attend_backward(query, key_rot, value, log_sums, grad_mixed)
    grad_projected = jnp.stack(
        [unrotate(grad_query, cosine, sine), unrotate(grad_key, cosine, sine), grad_value], axis=1
    )
    return grad_projected.reshape(rows, -1).astype(jnp.bfloat16)


def grid_plan(
    layer_input, gain_one, gain_two, query_key_value_weight, w_out, w_in, w_down, cotangent
):
    part_rows = query_key_value_weight.shape[0]
    heads_here = query_key_value_weight.shape[2] // HD
    residual_in = layer_input.astype(jnp.float32)
    centred_one, rstd_one = norm_forward(residual_in)
    first_normalized = (centred_one * gain_one).astype(jnp.bfloat16)
    gathered_one = widen_col(first_normalized)
    qkv_weight = query_key_value_weight.reshape(part_rows, -1)
    attention_projected = project_row(gathered_one, qkv_weight)
    rows = attention_projected.shape[0]
    mixed_low, kept = attention_part(attention_projected, rows, heads_here)
    gathered_mix = widen_row(mixed_low)
    middle = residual_in + project_col(gathered_mix, w_out)
    centred_two, rstd_two = norm_forward(middle)
    second_normalized = (centred_two * gain_two).astype(jnp.bfloat16)
    gathered_two = widen_col(second_normalized)
    in_weight = w_in.reshape(part_rows, -1)
    gate_up_output = project_row(gathered_two, in_weight).reshape(rows, 2, -1)
    hidden, gating_pull = jax.vjp(gating, gate_up_output)
    hidden_low = hidden.astype(jnp.bfloat16)
    gathered_hidden = widen_row(hidden_low)
    output = middle + project_col(gathered_hidden, w_down)
    down_grads = widen_col(cotangent)
    grad_hidden = return_row(down_grads, w_down)
    grad_w_down = weight_grad(gathered_hidden, down_grads)
    grad_gate_up = gating_pull(grad_hidden)[0].reshape(rows, -1).astype(jnp.bfloat16)
    in_grads = widen_row(grad_gate_up)
    grad_normed_two = return_col(in_grads, in_weight)
    grad_w_in = weight_grad(gathered_two, in_grads).reshape(w_in.shape)
    grad_norm_two, gain_part_two = norm_backward(grad_normed_two, centred_two, rstd_two, gain_two)
    grad_middle = cotangent.astype(jnp.float32) + grad_norm_two
    branch_grads = widen_col(grad_middle.astype(jnp.bfloat16))
    grad_mixed = return_row(branch_grads, w_out).astype(jnp.bfloat16)
    grad_w_out = weight_grad(gathered_mix, branch_grads)
    grad_projected = attention_back(grad_mixed, kept, rows, heads_here)
    proj_grads = widen_row(grad_projected)
    gradient_first_normalized = return_col(proj_grads, qkv_weight)
    grad_w_qkv = weight_grad(gathered_one, proj_grads).reshape(query_key_value_weight.shape)
    grad_norm_one, gain_part_one = norm_backward(
        gradient_first_normalized, centred_one, rstd_one, gain_one
    )
    grad_input = grad_middle + grad_norm_one
    grad_w_qkv, grad_w_out, grad_w_in, grad_w_down, gain_part_one, gain_part_two = sum_data(
        (grad_w_qkv, grad_w_out, grad_w_in, grad_w_down, gain_part_one, gain_part_two)
    )
    grad_gain_one, grad_gain_two = lax.psum((gain_part_one, gain_part_two), "col")
    return (
        output.astype(jnp.bfloat16),
        grad_input.astype(jnp.bfloat16),
        grad_w_qkv,
        grad_w_out,
        grad_w_in,
        grad_w_down,
        grad_gain_one,
        grad_gain_two,
    )


def per_device(
    layer_input, gain_one, gain_two, query_key_value_weight, w_out, w_in, w_down, cotangent
):
    return grid_plan(
        layer_input, gain_one, gain_two, query_key_value_weight, w_out, w_in, w_down, cotangent
    )


def solution(mesh):
    in_specs = (
        P(("dp", "col"), "row"),
        P("row"),
        P("row"),
        P("row", None, "col"),
        P("col", "row"),
        P("row", None, "col"),
        P("col", "row"),
        P(("dp", "col"), "row"),
    )
    out_specs = (
        P(("dp", "col"), "row"),
        P(("dp", "col"), "row"),
        P("row", None, "col"),
        P("col", "row"),
        P("row", None, "col"),
        P("col", "row"),
        P("row"),
        P("row"),
    )
    return jax.shard_map(
        per_device, mesh=mesh, in_specs=in_specs, out_specs=out_specs, check_vma=False
    )
```

profile of v0, /device:TPU:0, one launch (start us, length us, event | category | flops | bytes accessed | tf_op | source)
XLA Modules:
  0.0 4363.4 jit_solution(12451811206817646990)
XLA Ops:
  10.1 12.9 all-reduce.6
  27.4 149.8 %all-gather.9.cloned.1.call-done = bf16[16384,256]{1,0:T(8,128)(2,1)} async-done(((bf16[4096,256]{1,0:T(8,128)(2,1)}), bf16[16384,256]{1,0:T(8,128)(2,1)}) %all-gather.9.cloned.1.call-update) | async-done | bytes 8388624 | tf_op jit(solution)/shard_map/all_gather | solution.py:67
  177.2 21.7 fusion.96
  203.9 336.6 %reduce-scatter.9.cloned.1.call-done = f32[4096,768]{1,0:T(8,128)} async-done(((f32[16384,768]{1,0:T(8,128)}), f32[4096,768]{1,0:T(8,128)}) %reduce-scatter.9.cloned.1.call-update) | async-done | bytes 12582928 | tf_op jit(solution)/shard_map/reduce_scatter | solution.py:80
  540.5 12.6 copy.22
  565.3 6.2 fusion.80
  571.4 80.4 %while.30 = (s32[]{:T(128)}, bf16[8,512,4,64]{1,3,2,0:T(8,128)(2,1)}, f32[8,4,512]{2,1,0:T(4,128)}, s32[8]{0:T(128)S(1)}, bf16[4096,4,64]{0,2,1:T(8,128)(2,1)}, ...) while((s32[]{:T(128)}, ...), condition=%wide.region_8.9_spmd, body=%wide.region_5.8_spmd.sunk | while | flops 555743232 | bytes 27067788 | solution.py:161
  657.8 58.2 %all-gather.11.cloned.1.call-done = bf16[16384,256]{0,1:T(8,128)(2,1)} async-done(((bf16[4096,256]{0,1:T(8,128)(2,1)}), bf16[16384,256]{0,1:T(8,128)(2,1)}) %all-gather.11.cloned.1.call-update) | async-done | bytes 8388624 | tf_op jit(solution)/shard_map/all_gather | solution.py:71
  716.0 11.5 fusion.97
  728.2 279.8 %reduce-scatter.11.cloned.1.call-done = f32[4096,256]{1,0:T(8,128)} async-done(((f32[16384,256]{1,0:T(8,128)}), f32[4096,256]{1,0:T(8,128)}) %reduce-scatter.11.cloned.1.call-update) | async-done | bytes 4194320 | tf_op jit(solution)/shard_map/reduce_scatter | solution.py:91
  1008.0 4.7 fusion.92
  1012.8 11.1 all-reduce.5
  1028.4 131.5 %all-gather.17.cloned.1.call-done = bf16[16384,256]{1,0:T(8,128)(2,1)} async-done(((bf16[4096,256]{1,0:T(8,128)(2,1)}), bf16[16384,256]{1,0:T(8,128)(2,1)}) %all-gather.17.cloned.1.call-update) | async-done | bytes 8388624 | tf_op jit(solution)/shard_map/all_gather | solution.py:67
  1159.9 21.9 fusion.100
  1181.9 127.9 %all-gather.13.cloned.1.call-done = bf16[16384,256]{1,0:T(8,128)(2,1)} async-done(((bf16[4096,256]{1,0:T(8,128)(2,1)}), bf16[16384,256]{1,0:T(8,128)(2,1)}) %all-gather.13.cloned.1.call-update) | async-done | bytes 8388624 | tf_op jit(solution)/shard_map/all_gather | solution.py:67
  1309.8 54.9 %fusion.98 = f32[16384,1312]{0,1:T(8,128)} fusion(bf16[16384,256]{1,0:T(8,128)(2,1)} %all-gather.13.cloned.1.call-done, bf16[256,1312]{0,1:T(8,128)(2,1)S(1)} %bitcast.199), kind=kOutput, calls=%fused_computation.159 | convolution fusion | flops 11005853696 | bytes 95043584 | tf_op jit(solution)/shard_map/dot_general | solution.py:78
  1365.1 241.1 %reduce-scatter.17.cloned.1.call-done = f32[4096,656]{0,1:T(8,128)} async-done(((f32[16384,656]{0,1:T(8,128)}), f32[4096,656]{0,1:T(8,128)}) %reduce-scatter.17.cloned.1.call-update) | async-done | bytes 10747920 | tf_op jit(solution)/shard_map/reduce_scatter | solution.py:104
  1606.2 576.4 %reduce-scatter.13.cloned.1.call-done = f32[4096,1312]{0,1:T(8,128)} async-done(((f32[16384,1312]{0,1:T(8,128)}), f32[4096,1312]{0,1:T(8,128)}) %reduce-scatter.13.cloned.1.call-update) | async-done | bytes 21495824 | tf_op jit(solution)/shard_map/reduce_scatter | solution.py:80
  2182.6 26.6 multiply_bitcast_fusion
  2209.2 14.9 fusion.51
  2224.1 11.8 add_convert_fusion
  2236.6 255.7 %all-gather.19.cloned.1.call-done = bf16[16384,1312]{0,1:T(8,128)(2,1)} async-done(((bf16[4096,1312]{0,1:T(8,128)(2,1)}), bf16[16384,1312]{0,1:T(8,128)(2,1)}) %all-gather.19.cloned.1.call-update) | async-done | bytes 42991632 | tf_op jit(solution)/shard_map/all_gather | solution.py:71
  2492.3 28.5 fusion.101
  2521.0 107.3 %all-gather.15.cloned.1.call-done = bf16[16384,656]{0,1:T(8,128)(2,1)} async-done(((bf16[4096,656]{0,1:T(8,128)(2,1)}), bf16[16384,656]{0,1:T(8,128)(2,1)}) %all-gather.15.cloned.1.call-update) | async-done | bytes 21495824 | tf_op jit(solution)/shard_map/all_gather | solution.py:71
  2628.3 14.4 fusion.99
  2642.8 268.2 %reduce-scatter.19.cloned.1.call-done = f32[4096,256]{1,0:T(8,128)} async-done(((f32[16384,256]{1,0:T(8,128)}), f32[4096,256]{1,0:T(8,128)}) %reduce-scatter.19.cloned.1.call-update) | async-done | bytes 4194320 | tf_op jit(solution)/shard_map/reduce_scatter | solution.py:117
  2911.0 5.2 multiply_reduce_fusion.2
  2916.2 11.3 all-reduce.4
  2927.5 266.8 %reduce-scatter.15.cloned.1.call-done = f32[4096,256]{1,0:T(8,128)} async-done(((f32[16384,256]{1,0:T(8,128)}), f32[4096,256]{1,0:T(8,128)}) %reduce-scatter.15.cloned.1.call-update) | async-done | bytes 4194320 | tf_op jit(solution)/shard_map/reduce_scatter | solution.py:91
  3194.4 8.9 fusion.93
  3203.3 150.5 %all-gather.21.cloned.1.call-done = bf16[16384,256]{1,0:T(8,128)(2,1)} async-done(((bf16[4096,256]{1,0:T(8,128)(2,1)}), bf16[16384,256]{1,0:T(8,128)(2,1)}) %all-gather.21.cloned.1.call-update) | async-done | bytes 8388624 | tf_op jit(solution)/shard_map/all_gather | solution.py:67
  3353.8 11.6 fusion.102
  3365.6 124.2 %reduce-scatter.21.cloned.1.call-done = f32[4096,256]{1,0:T(8,128)} async-done(((f32[16384,256]{1,0:T(8,128)}), f32[4096,256]{1,0:T(8,128)}) %reduce-scatter.21.cloned.1.call-update) | async-done | bytes 4194320 | tf_op jit(solution)/shard_map/reduce_scatter | solution.py:104
  3502.8 283.0 %while.31 = (s32[]{:T(128)}, f32[4096,4,64]{0,2,1:T(8,128)}, f32[4096,4,64]{0,2,1:T(8,128)}, f32[8,512,4,64]{1,0,3,2:T(8,128)}, s32[8]{0:T(128)S(1)}, /*index=5*...) while((s32[]{:T(128)}, f32[4096,4,64]{0,2,1:T(8,128)}, ...), condition=%wide.region_25.26_spmd, body=%wide.region_23.25_spmd.sunk | while | flops 1368258560 | bytes 156295712 | solution.py:212
  3517.3 11.5 dynamic_update_slice.45
  3528.8 4.6 fusion.157
  3552.6 11.5 dynamic_update_slice.45
  3564.1 4.6 fusion.157
  3588.0 11.5 dynamic_update_slice.45
  3599.5 4.7 fusion.157
  3623.4 11.5 dynamic_update_slice.45
  3634.9 4.7 fusion.157
  3658.8 11.5 dynamic_update_slice.45
  3670.3 4.6 fusion.157
  3694.1 11.5 dynamic_update_slice.45
  3705.7 4.6 fusion.157
  3729.5 11.5 dynamic_update_slice.45
  3741.0 4.6 fusion.157
  3764.9 11.5 dynamic_update_slice.45
  3776.4 4.6 fusion.157
  3785.8 4.9 reshape.215
  3790.8 5.5 reshape.214
  3812.8 16.2 convolution_convert_fusion.2
  3829.0 25.5 convolution_convert_fusion
  3854.5 8.8 convolution_convert_fusion.3
  3863.3 104.4 %all-gather.23.cloned.1.call-done = bf16[16384,768]{0,1:T(8,128)(2,1)} async-done(((bf16[4096,768]{0,1:T(8,128)(2,1)}), bf16[16384,768]{0,1:T(8,128)(2,1)}) %all-gather.23.cloned.1.call-update) | async-done | bytes 25165840 | tf_op jit(solution)/shard_map/all_gather | solution.py:71
  3967.7 14.3 convolution_convert_fusion.1
  3983.0 15.4 fusion.103
  3998.5 35.7 all-reduce.11.cloned.1.call-done
  4042.0 275.1 %reduce-scatter.23.cloned.1.call-done = f32[4096,256]{1,0:T(8,128)} async-done(((f32[16384,256]{1,0:T(8,128)}), f32[4096,256]{1,0:T(8,128)}) %reduce-scatter.23.cloned.1.call-update) | async-done | bytes 4194320 | tf_op jit(solution)/shard_map/reduce_scatter | solution.py:117
  4321.1 10.9 all-reduce.3
  4332.1 4.9 all-reduce.7
  4337.0 12.4 all-reduce.2
  4349.4 7.3 fusion.74
  (291 shorter events, 302.5 us)
Async XLA Ops:
  7.2 1302.6 %copy-start = (bf16[256,2,656]{0,2,1:T(8,128)(2,1)S(1)}, bf16[256,2,656]{0,2,1:T(8,128)(2,1)}, u32[]{:S(2)}) copy-start(bf16[256,2,656]{0,2,1:T(8,128)(2,1)} %param.17) | copy-start | bytes 2015236
  7.2 20.0 copy-start.21
  7.2 170.0 %all-gather.9.cloned.1.call-start = ((), (), s32[]{:S(2)}) async-start(), calls=%async_computation.8 | async-start | bytes 10485760 | tf_op jit(solution)/shard_map/all_gather | solution.py:67
  27.1 513.4 %reduce-scatter.9.cloned.1.call-start = ((), (), s32[]{:S(2)}) async-start(), calls=%async_computation.9 | async-start | bytes 62914560 | tf_op jit(solution)/shard_map/reduce_scatter | solution.py:80
  27.3 171.6 %copy-start.17 = (bf16[256,3,256]{0,2,1:T(8,128)(2,1)}, bf16[256,3,256]{0,2,1:T(8,128)(2,1)S(1)}, u32[]{:S(2)}) copy-start(bf16[256,3,256]{0,2,1:T(8,128)(2,1)S(1)} %copy.21) | copy-start | bytes 1179652
  199.0 517.1 %all-gather.11.cloned.1.call-start = ((), (), s32[]{:S(2)}) async-start(), calls=%async_computation.10 | async-start | bytes 10485760 | tf_op jit(solution)/shard_map/all_gather | solution.py:71
  553.1 7.0 copy-start.5
  651.8 75.8 %copy-start.10 = (bf16[4096,4,64]{0,2,1:T(8,128)(2,1)}, bf16[4096,4,64]{0,2,1:T(8,128)(2,1)S(1)}, u32[]{:S(2)}) copy-start(bf16[4096,4,64]{0,2,1:T(8,128)(2,1)S(1)} %get-tuple-element.588) | copy-start | bytes 6291460
  651.8 64.2 %copy-start.19 = (bf16[256,256]{1,0:T(8,128)(2,1)S(1)}, bf16[256,256]{1,0:T(8,128)(2,1)}, u32[]{:S(2)}) copy-start(bf16[256,256]{1,0:T(8,128)(2,1)} %param.16) | copy-start | bytes 393220
  657.6 350.5 %reduce-scatter.11.cloned.1.call-start = ((), (), s32[]{:S(2)}) async-start(), calls=%async_computation.11 | async-start | bytes 20971520 | tf_op jit(solution)/shard_map/reduce_scatter | solution.py:91
  727.6 280.5 %copy-start.7 = (bf16[4096,256]{1,0:T(8,128)(2,1)S(1)}, bf16[4096,256]{1,0:T(8,128)(2,1)}, u32[]{:S(2)}) copy-start(bf16[4096,256]{1,0:T(8,128)(2,1)} %param.12) | copy-start | bytes 6291460
  727.6 296.9 %copy-start.31 = (f32[256]{0:T(256)S(1)}, f32[256]{0:T(256)}, u32[]{:S(2)}) copy-start(f32[256]{0:T(256)} %param.14) | copy-start | bytes 3076
  727.6 432.3 %all-gather.17.cloned.1.call-start = ((), (), s32[]{:S(2)}) async-start(), calls=%async_computation.16 | async-start | bytes 10485760 | tf_op jit(solution)/shard_map/all_gather | solution.py:67
  728.2 581.6 %all-gather.13.cloned.1.call-start = ((), (), s32[]{:S(2)}) async-start(), calls=%async_computation.12 | async-start | bytes 10485760 | tf_op jit(solution)/shard_map/all_gather | solution.py:67
  1012.8 147.1 %copy-start.22 = (bf16[656,256]{1,0:T(8,128)(2,1)S(1)}, bf16[656,256]{1,0:T(8,128)(2,1)}, u32[]{:S(2)}) copy-start(bf16[656,256]{1,0:T(8,128)(2,1)} %param.18) | copy-start | bytes 1007620
  1028.3 577.8 %reduce-scatter.17.cloned.1.call-start = ((), (), s32[]{:S(2)}) async-start(), calls=%async_computation.17 | async-start | bytes 53739520 | tf_op jit(solution)/shard_map/reduce_scatter | solution.py:104
  1181.8 1000.7 %reduce-scatter.13.cloned.1.call-start = ((), (), s32[]{:S(2)}) async-start(), calls=%async_computation.13 | async-start | bytes 107479040 | tf_op jit(solution)/shard_map/reduce_scatter | solution.py:80
  1364.7 1127.7 %all-gather.19.cloned.1.call-start = ((), (), s32[]{:S(2)}) async-start(), calls=%async_computation.18 | async-start | bytes 53739520 | tf_op jit(solution)/shard_map/all_gather | solution.py:71
  2182.6 26.6 copy-start.9
  2235.9 392.3 %all-gather.15.cloned.1.call-start = ((), (), s32[]{:S(2)}) async-start(), calls=%async_computation.14 | async-start | bytes 26869760 | tf_op jit(solution)/shard_map/all_gather | solution.py:71
  2236.5 674.5 %reduce-scatter.19.cloned.1.call-start = ((), (), s32[]{:S(2)}) async-start(), calls=%async_computation.19 | async-start | bytes 20971520 | tf_op jit(solution)/shard_map/reduce_scatter | solution.py:117
  2520.8 673.6 %reduce-scatter.15.cloned.1.call-start = ((), (), s32[]{:S(2)}) async-start(), calls=%async_computation.15 | async-start | bytes 20971520 | tf_op jit(solution)/shard_map/reduce_scatter | solution.py:91
  2642.7 268.3 %copy-start.28 = (f32[4096]{0:T(1024)S(1)}, f32[4096]{0:T(1024)}, u32[]{:S(2)}) copy-start(f32[4096]{0:T(1024)} %copy-done.27) | copy-start | bytes 49156
  2642.7 268.3 %copy-start.30 = (f32[4096]{0:T(1024)S(1)}, f32[4096]{0:T(1024)}, u32[]{:S(2)}) copy-start(f32[4096]{0:T(1024)} %copy-done.29) | copy-start | bytes 49156
  2642.7 268.3 %copy-start.32 = (f32[256]{0:T(256)S(1)}, f32[256]{0:T(256)}, u32[]{:S(2)}) copy-start(f32[256]{0:T(256)} %param.14) | copy-start | bytes 3076
  2642.7 551.7 %copy-start.16 = (bf16[4096,256]{1,0:T(8,128)(2,1)S(1)}, bf16[4096,256]{1,0:T(8,128)(2,1)}, u32[]{:S(2)}) copy-start(bf16[4096,256]{1,0:T(8,128)(2,1)} %param.19) | copy-start | bytes 6291460
  2642.7 711.1 %all-gather.21.cloned.1.call-start = ((), (), s32[]{:S(2)}) async-start(), calls=%async_computation.20 | async-start | bytes 10485760 | tf_op jit(solution)/shard_map/all_gather | solution.py:67
  2927.5 426.3 %copy-start.20 = (bf16[256,256]{1,0:T(8,128)(2,1)S(1)}, bf16[256,256]{1,0:T(8,128)(2,1)}, u32[]{:S(2)}) copy-start(bf16[256,256]{1,0:T(8,128)(2,1)} %param.16) | copy-start | bytes 393220
  3203.3 286.6 %reduce-scatter.21.cloned.1.call-start = ((), (), s32[]{:S(2)}) async-start(), calls=%async_computation.21 | async-start | bytes 20971520 | tf_op jit(solution)/shard_map/reduce_scatter | solution.py:104
  3365.4 602.3 %all-gather.23.cloned.1.call-start = ((), (), s32[]{:S(2)}) async-start(), calls=%async_computation.22 | async-start | bytes 31457280 | tf_op jit(solution)/shard_map/all_gather | solution.py:71
  3493.6 9.2 copy-start.11
  3506.3 4.9 copy-start.2
  3513.2 2.1 copy-start.4
  3528.8 5.4 copy-start.3
  3541.7 4.9 copy-start.2
  3548.6 2.1 copy-start.4
  3564.1 5.4 copy-start.3
  3577.0 4.9 copy-start.2
  3584.0 2.1 copy-start.4
  3599.5 5.4 copy-start.3
  3612.4 4.9 copy-start.2
  3634.9 5.4 copy-start.3
  3647.8 4.9 copy-start.2
  3670.3 5.4 copy-start.3
  3683.2 4.9 copy-start.2
  3705.6 5.4 copy-start.3
  3718.6 4.9 copy-start.2
  3741.0 5.4 copy-start.3
  3754.0 4.9 copy-start.2
  3776.4 5.4 copy-start.3
  3790.8 5.5 copy-start.15
  3800.9 3.0 copy-start.12
  3800.9 4.2 copy-start.6
  3800.9 4.4 copy-start.14
  3804.1 4.0 copy-start.13
  3812.7 221.5 %all-reduce.11.cloned.1.call-start = ((), (), s32[]{:S(2)}) async-start(), calls=%async_computation.24 | async-start | bytes 3063808 | tf_op jit(solution)/shard_map/psum | solution.py:130
  3863.3 119.7 %copy-start.18 = (bf16[256,3,256]{0,2,1:T(8,128)(2,1)S(1)}, bf16[256,3,256]{0,2,1:T(8,128)(2,1)}, u32[]{:S(2)}) copy-start(bf16[256,3,256]{0,2,1:T(8,128)(2,1)} %copy-done.17) | copy-start | bytes 1179652
  3983.0 334.1 %reduce-scatter.23.cloned.1.call-start = ((), (), s32[]{:S(2)}) async-start(), calls=%async_computation.23 | async-start | bytes 20971520 | tf_op jit(solution)/shard_map/reduce_scatter | solution.py:117
  3998.4 318.7 %copy-start.8 = (bf16[4096,256]{1,0:T(8,128)(2,1)S(1)}, bf16[4096,256]{1,0:T(8,128)(2,1)}, u32[]{:S(2)}) copy-start(bf16[4096,256]{1,0:T(8,128)(2,1)} %param.12) | copy-start | bytes 6291460
  3998.4 318.7 %copy-start.24 = (f32[4096]{0:T(1024)S(1)}, f32[4096]{0:T(1024)}, u32[]{:S(2)}) copy-start(f32[4096]{0:T(1024)} %copy-done.23) | copy-start | bytes 49156
  3998.4 318.7 %copy-start.26 = (f32[4096]{0:T(1024)S(1)}, f32[4096]{0:T(1024)}, u32[]{:S(2)}) copy-start(f32[4096]{0:T(1024)} %copy-done.25) | copy-start | bytes 49156
  3998.4 318.7 %copy-start.33 = (f32[256]{0:T(256)S(1)}, f32[256]{0:T(256)}, u32[]{:S(2)}) copy-start(f32[256]{0:T(256)} %param.13) | copy-start | bytes 3076
  3998.5 333.6 %copy-start.34 = (bf16[256]{0:T(256)(128)(2,1)S(1)}, bf16[256]{0:T(256)(128)(2,1)}, u32[]{:S(2)}) copy-start(bf16[256]{0:T(256)(128)(2,1)} %get-tuple-element.250) | copy-start | bytes 1540
  4349.4 7.3 copy-start.1
  (9 other events, 12.8 us)
Sparse Core Ops, SparseCore 0:
  27.2 149.9 all-gather.8
  199.1 341.3 reduce-scatter.8
  657.7 58.2 all-gather.10
  727.7 280.2 reduce-scatter.10
  1009.5 150.3 all-gather.16
  1161.9 147.8 all-gather.12
  1312.4 293.7 reduce-scatter.16
  1609.0 573.5 reduce-scatter.12
  2236.1 256.2 all-gather.18
  2493.7 134.5 all-gather.14
  2630.7 280.2 reduce-scatter.18
  2913.3 281.0 reduce-scatter.14
  3203.4 150.3 all-gather.20
  3365.5 124.3 reduce-scatter.20
  3812.9 154.7 all-gather.22
  3983.1 51.0 all-reduce.10
  4036.5 280.5 reduce-scatter.22
where the time goes:
time: 4370 us; the launch traced here: 4360 us
  waiting for transfers between devices  3490 us (80%)
  matrix products  427 us (10%)
  local copies, waits for them, and re-layouts  188 us (4%)
  other arithmetic  167 us (4%)
  blocking collectives  63.5 us (1%)
    reduce_scatter x2, waiting for transfers between devices, project_row(): lax.psum_scatter(term(jnp.int32(0), rows * lax.axis_size('row')), 'row',...  913 us
    all_gather x4, waiting for transfers between devices, widen_col(): return lax.all_gather(values, 'col', axis=0, tiled=True)  560 us
    reduce_scatter x2, waiting for transfers between devices, project_col(): lax.psum_scatter(term(jnp.int32(0), rows * lax.axis_size('col')), 'col',...  547 us
    reduce_scatter x2, waiting for transfers between devices, return_col(): lax.psum_scatter(term(jnp.int32(0), rows * lax.axis_size('col')), 'col',...  543 us
    all_gather x4, waiting for transfers between devices, widen_row(): return lax.all_gather(values, 'row', axis=0, tiled=True)  526 us
    reduce_scatter x2, waiting for transfers between devices, return_row(): lax.psum_scatter(term(jnp.int32(0), rows * lax.axis_size('row')), 'row',...  365 us
    dot_general x4, matrix products, term(): return jnp.dot(gathered, weight, preferred_element_type=jnp.float32)  102 us
    dynamic_update_slice x16, local copies, waits for them, and re-layouts, attend_forward(): results, log_sums = lax.map(one_block, jnp.arange(rows // block))  96.3 us
  transfers between devices with their start and end apart: 17, of which 17 were waited for; matrix products, arithmetic and copies ran while one was open for 5% of the time, Pallas kernels for 0%

commit v1 on v0

v1 whole, which is shorter than its diff:
```python
import functools

import jax
import jax.numpy as jnp
from jax import lax
from jax.experimental import pallas as pl
from jax.experimental.pallas import tpu as pltpu
from jax.sharding import PartitionSpec as P

HD = 64
LEN = 1024
PAIR = 2 * HD
CHUNK = 512

EPSILON = 1e-05
THETA = 160000.0
BOTH = ("col", "row")
VMEM = 56 * 1024 * 1024


def turning(size):
    positions = jnp.arange(LEN).astype(jnp.float32)
    inverse = THETA ** (-jnp.arange(0, size, 2, dtype=jnp.float32) / size)
    phase = positions[:, None] * inverse[None, :]
    phase = jnp.concatenate([phase] * (2 * PAIR // size), axis=-1)
    return (jnp.cos(phase), jnp.sin(phase))


def first_half(shape):
    lane = lax.broadcasted_iota(jnp.int32, shape, len(shape) - 1)
    return lane % HD < HD // 2


def turn(values):
    ahead = pltpu.roll(values, PAIR - HD // 2, 1)
    behind = pltpu.roll(values, HD // 2, 1)
    return jnp.where(first_half(values.shape), -ahead, behind)


def unturn(values):
    ahead = pltpu.roll(values, PAIR - HD // 2, 1)
    behind = pltpu.roll(values, HD // 2, 1)
    return jnp.where(first_half(values.shape), ahead, -behind)


def dot(left, right, over):
    return lax.dot_general(left, right, (over, ((), ())), preferred_element_type=jnp.float32)


def attend_kernel(q_ref, k_ref, v_ref, cos_ref, sin_ref, qo_ref, ko_ref, vo_ref, mixed_ref):
    cosine, sine = cos_ref[...], sin_ref[...]
    query = q_ref[0]
    query = (query * cosine + turn(query) * sine).astype(jnp.bfloat16)
    key = k_ref[0]
    key = (key * cosine + turn(key) * sine).astype(jnp.bfloat16)
    value = v_ref[0].astype(jnp.bfloat16)
    qo_ref[...] = query
    ko_ref[...] = key
    vo_ref[...] = value
    scale = HD ** (-0.5)
    for start in range(0, LEN, CHUNK):
        parts = []
        for head in range(2):
            lanes = slice(head * HD, head * HD + HD)
            scores = dot(query[start : start + CHUNK, lanes], key[:, lanes], ((1,), (1,)))
            top = jnp.max(scores, axis=-1, keepdims=True)
            exponent = jnp.exp((scores - top) * scale)
            total = jnp.sum(exponent, axis=-1, keepdims=True)
            part = dot(exponent.astype(jnp.bfloat16), value[:, lanes], ((1,), (0,)))
            parts.append(part / total)
        mixed_ref[start : start + CHUNK, :] = jnp.concatenate(parts, axis=1).astype(jnp.bfloat16)


def attend_back_kernel(q_ref, k_ref, v_ref, do_ref, cos_ref, sin_ref, dq_ref, dk_ref, dv_ref):
    scale = HD ** (-0.5)
    dqs, dks, dvs = [], [], []
    for head in range(2):
        lanes = slice(head * HD, head * HD + HD)
        key = k_ref[:, lanes]
        value = v_ref[:, lanes]
        dq_parts, dk, dv = [], None, None
        for start in range(0, LEN, CHUNK):
            query = q_ref[start : start + CHUNK, lanes]
            grad = do_ref[start : start + CHUNK, lanes]
            scores = dot(key, query, ((1,), (1,)))
            top = jnp.max(scores, axis=0, keepdims=True)
            exponent = jnp.exp((scores - top) * scale)
            probs = exponent * (1.0 / jnp.sum(exponent, axis=0, keepdims=True))
            value_part = dot(probs.astype(jnp.bfloat16), grad, ((1,), (0,)))
            grad_probs = dot(value, grad, ((1,), (1,)))
            inner = jnp.sum(probs * grad_probs, axis=0, keepdims=True)
            grad_scores = (probs * (grad_probs - inner)).astype(jnp.bfloat16)
            key_part = dot(grad_scores, query, ((1,), (0,)))
            dq_parts.append(dot(grad_scores, key, ((0,), (0,))))
            dk = key_part if dk is None else dk + key_part
            dv = value_part if dv is None else dv + value_part
        dqs.append(jnp.concatenate(dq_parts, axis=0))
        dks.append(dk)
        dvs.append(dv)
    cosine, sine = cos_ref[...], sin_ref[...]
    dq = jnp.concatenate(dqs, axis=1) * scale
    dk = jnp.concatenate(dks, axis=1) * scale
    dq_ref[0] = (dq * cosine + unturn(dq * sine)).astype(jnp.bfloat16)
    dk_ref[0] = (dk * cosine + unturn(dk * sine)).astype(jnp.bfloat16)
    dv_ref[0] = jnp.concatenate(dvs, axis=1).astype(jnp.bfloat16)


def attend_forward(projected, cosine, sine):
    cols, rows, width = projected.shape
    pairs = width // 3 // PAIR

    def wide(which):
        return pl.BlockSpec(
            (1, LEN, PAIR), lambda s, c, p, which=which: (c, s, which * pairs + p)
        )

    angle = pl.BlockSpec((LEN, PAIR), lambda s, c, p: (0, 0))
    flat = pl.BlockSpec((LEN, PAIR), lambda s, c, p: (s, c * pairs + p))
    shape = jax.ShapeDtypeStruct((rows, cols * pairs * PAIR), jnp.bfloat16)
    return pl.pallas_call(
        attend_kernel,
        grid=(rows // LEN, cols, pairs),
        in_specs=[wide(0), wide(1), wide(2), angle, angle],
        out_specs=[flat] * 4,
        out_shape=[shape] * 4,
        compiler_params=pltpu.CompilerParams(vmem_limit_bytes=VMEM),
        name="attend_forward",
    )(projected, projected, projected, cosine, sine)


def attend_backward(query, key, value, grad_mixed, cosine, sine, cols):
    rows, width = query.shape
    pairs = width // cols // PAIR
    angle = pl.BlockSpec((LEN, PAIR), lambda s, c, p: (0, 0))
    flat = pl.BlockSpec((LEN, PAIR), lambda s, c, p: (s, c * pairs + p))
    out = pl.BlockSpec((1, LEN, PAIR), lambda s, c, p: (c, s, p))
    shape = jax.ShapeDtypeStruct((cols, rows, pairs * PAIR), jnp.bfloat16)
    parts = pl.pallas_call(
        attend_back_kernel,
        grid=(rows // LEN, cols, pairs),
        in_specs=[flat] * 4 + [angle] * 2,
        out_specs=[out] * 3,
        out_shape=[shape] * 3,
        compiler_params=pltpu.CompilerParams(vmem_limit_bytes=VMEM),
        name="attend_backward",
    )(query, key, value, grad_mixed, cosine, sine)
    return jnp.concatenate(parts, axis=2)


def norm_forward(values):
    mean = jnp.mean(values, axis=1, keepdims=True)
    square = jnp.mean(values * values, axis=1, keepdims=True)
    rstd = lax.rsqrt(square - mean * mean + EPSILON)
    return ((values - mean) * rstd, rstd)


def norm_backward(grads, centred, rstd, gain):
    scaled = grads * gain
    first = jnp.mean(scaled, axis=1, keepdims=True)
    second = jnp.mean(scaled * centred, axis=1, keepdims=True)
    result = rstd * (scaled - first - centred * second)
    return (result, jnp.sum(grads * centred, axis=0))


def gather(block):
    return lax.all_gather(block, BOTH, axis=0, tiled=False)


def scatter(blocks):
    return lax.psum_scatter(blocks.astype(jnp.bfloat16), BOTH, scatter_dimension=0, tiled=False)


def per_device(
    layer_input, gain_one, gain_two, query_key_value_weight, w_out, w_in, w_down, cotangent
):
    cols, rows_axis = lax.axis_size("col"), lax.axis_size("row")
    part = query_key_value_weight.shape[0]
    width = part * rows_axis
    hid = w_down.shape[0]
    f32, bf16 = jnp.float32, jnp.bfloat16

    residual_low = lax.all_to_all(layer_input, "row", 0, 1, tiled=True)
    gains = lax.all_gather(jnp.stack([gain_one, gain_two]), "row", axis=1, tiled=True)
    full_one, full_two = gains[0], gains[1]
    qkv = gather(query_key_value_weight.reshape(part, -1)).reshape(cols, width, -1)
    out = gather(w_out).reshape(cols, rows_axis, part, part)
    gate_w = gather(w_in[:, 0]).reshape(cols, width, hid)
    up_w = gather(w_in[:, 1]).reshape(cols, width, hid)
    down = gather(w_down).reshape(cols, rows_axis, hid, part)
    down = jnp.swapaxes(down, 1, 2).reshape(cols, hid, width)
    out = jnp.swapaxes(out, 1, 2).reshape(width, width)
    grad_out = lax.all_to_all(cotangent, "row", 0, 1, tiled=True)

    residual_in = residual_low.astype(f32)
    rows = residual_in.shape[0]
    cosine, sine = turning(HD)
    centred_one, rstd_one = norm_forward(residual_in)
    normed_one = (centred_one * full_one).astype(bf16)
    projected = jnp.einsum("td,cdn->ctn", normed_one, qkv, preferred_element_type=f32)
    query, key, value, mixed = attend_forward(projected, cosine, sine)
    middle = residual_in + jnp.dot(mixed, out, preferred_element_type=f32)
    centred_two, rstd_two = norm_forward(middle)
    normed_two = (centred_two * full_two).astype(bf16)
    gate = jnp.einsum("td,cdn->ctn", normed_two, gate_w, preferred_element_type=f32)
    up = jnp.einsum("td,cdn->ctn", normed_two, up_w, preferred_element_type=f32)
    hidden = (jax.nn.gelu(gate, approximate=False) * up).astype(bf16)
    output = middle + jnp.einsum("ctn,cnd->td", hidden, down, preferred_element_type=f32)
    output = lax.all_to_all(output.astype(bf16), "row", 1, 0, tiled=True)

    grad_hidden = jnp.einsum("td,cnd->ctn", grad_out, down, preferred_element_type=f32)
    grad_down = jnp.einsum("ctn,trd->crnd", hidden, grad_out.reshape(rows, rows_axis, part), preferred_element_type=f32)
    grad_down = scatter(grad_down.reshape(-1, hid, part))
    _, pull = jax.vjp(lambda g, u: jax.nn.gelu(g, approximate=False) * u, gate, up)
    grad_gate, grad_up = pull(grad_hidden)
    grad_gate, grad_up = grad_gate.astype(bf16), grad_up.astype(bf16)
    grad_gate_w = jnp.einsum("td,ctn->cdn", normed_two, grad_gate, preferred_element_type=f32)
    grad_gate_w = scatter(grad_gate_w.reshape(-1, part, hid))
    grad_up_w = jnp.einsum("td,ctn->cdn", normed_two, grad_up, preferred_element_type=f32)
    grad_up_w = scatter(grad_up_w.reshape(-1, part, hid))
    grad_normed_two = jnp.einsum(
        "ctn,cdn->td", grad_gate, gate_w, preferred_element_type=f32
    ) + jnp.einsum("ctn,cdn->td", grad_up, up_w, preferred_element_type=f32)
    grad_norm_two, gain_part_two = norm_backward(grad_normed_two, centred_two, rstd_two, full_two)
    grad_middle = grad_out.astype(f32) + grad_norm_two
    branch = grad_middle.astype(bf16)
    grad_mixed = dot(branch, out, ((1,), (1,))).astype(bf16)
    grad_w_out = jnp.einsum(
        "tcm,trd->crmd",
        mixed.reshape(rows, cols, part),
        branch.reshape(rows, rows_axis, part),
        preferred_element_type=f32,
    )
    grad_w_out = scatter(grad_w_out.reshape(-1, part, part))
    grad_projected = attend_backward(query, key, value, grad_mixed, cosine, sine, cols)
    grad_normed_one = jnp.einsum("ctn,cdn->td", grad_projected, qkv, preferred_element_type=f32)
    grad_qkv = jnp.einsum("td,ctn->cdn", normed_one, grad_projected, preferred_element_type=f32)
    grad_qkv = scatter(grad_qkv.reshape(-1, part, qkv.shape[2]))
    grad_norm_one, gain_part_one = norm_backward(
        grad_normed_one, centred_one, rstd_one, full_one
    )
    grad_input = (grad_middle + grad_norm_one).astype(bf16)
    grad_input = lax.all_to_all(grad_input, "row", 1, 0, tiled=True)

    sums = lax.psum((grad_down, grad_gate_w, grad_up_w, grad_w_out, grad_qkv), "dp")
    grad_down, grad_gate_w, grad_up_w, grad_w_out, grad_qkv = (s.astype(f32) for s in sums)
    gain_sums = lax.psum(jnp.stack([gain_part_one, gain_part_two]), ("dp", "col", "row"))
    mine = lax.dynamic_slice_in_dim(gain_sums, lax.axis_index("row") * part, part, 1)
    return (
        output,
        grad_input,
        grad_qkv.reshape(query_key_value_weight.shape),
        grad_w_out,
        jnp.stack([grad_gate_w, grad_up_w], axis=1),
        grad_down,
        mine[0],
        mine[1],
    )


def solution(mesh):
    in_specs = (
        P(("dp", "col"), "row"),
        P("row"),
        P("row"),
        P("row", None, "col"),
        P("col", "row"),
        P("row", None, "col"),
        P("col", "row"),
        P(("dp", "col"), "row"),
    )
    out_specs = (
        P(("dp", "col"), "row"),
        P(("dp", "col"), "row"),
        P("row", None, "col"),
        P("col", "row"),
        P("row", None, "col"),
        P("col", "row"),
        P("row"),
        P("row"),
    )
    return jax.shard_map(
        per_device, mesh=mesh, in_specs=in_specs, out_specs=out_specs, check_vma=False
    )
```

time: 4370 us -> 1050 us (0.24)
  waiting for transfers between devices: 3490 us -> 486 us
  matrix products: 427 us -> 169 us
  other arithmetic: 167 us -> 40.2 us
  Pallas kernels: 0 us -> 113 us
  local copies, waits for them, and re-layouts: 188 us -> 127 us
    reduce_scatter x8 -> x5, waiting for transfers between devices: 2370 us -> 265 us  [scatter(): lax.psum_scatter(blocks.astype(jnp.bfloat16), BOTH, scatter_dimension=0,...]
    all_gather x8 -> x5, waiting for transfers between devices: 1090 us -> 165 us  [gather(): return lax.all_gather(block, BOTH, axis=0, tiled=False)]
    dot_general x68 -> x15, matrix products: 427 us -> 169 us  [the longest x1 38.2 us: per_device(): up = jnp.einsum('td,cdn->ctn', normed_two, up_w, preferred_element_type=f32)]
    pallas_call x0 -> x2, Pallas kernels: none -> 113 us  [the longest x1 71.9 us: attend_backward(): pl.pallas_call(attend_back_kernel, grid=(rows // LEN, cols, pairs), in_sp...]
    dynamic_update_slice x16 -> x0, local copies, waits for them, and re-layouts: 96.3 us -> none  [attend_forward(): results, log_sums = lax.map(one_block, jnp.arange(rows // block))]
    convert_element_type x4 -> x9, local copies, waits for them, and re-layouts: 10.3 us -> 65.8 us  [the longest x8 60.4 us: scatter(): blocks.astype(jnp.bfloat16)]
    all_to_all x0 -> x4, waiting for transfers between devices: none -> 47.3 us  [the longest x1 27.6 us: per_device(): grad_out = lax.all_to_all(cotangent, 'row', 0, 1, tiled=True)]
  transfers between devices with their start and end apart: 17 -> 15, of which waited for: 17 -> 11; matrix products, arithmetic and copies ran while one was open for 5% -> 17% of each run, Pallas kernels for 0% -> 0%
where the time goes in v1:
time: 1050 us; the launch traced here: 1040 us
  waiting for transfers between devices  486 us (46%)
  matrix products  169 us (16%)
  local copies, waits for them, and re-layouts  127 us (12%)
  Pallas kernels  113 us (11%)
  blocking collectives  69.7 us (7%)
  other arithmetic  40.2 us (4%)
  starting transfers between devices  16.4 us (2%)
  between operations  14.7 us (1%)
    reduce_scatter x5, waiting for transfers between devices, scatter(): lax.psum_scatter(blocks.astype(jnp.bfloat16), BOTH, scatter_dimension=0,...  265 us
    all_gather x5, waiting for transfers between devices, gather(): return lax.all_gather(block, BOTH, axis=0, tiled=False)  165 us
    pallas_call x1, Pallas kernels, attend_backward(): pl.pallas_call(attend_back_kernel, grid=(rows // LEN, cols, pairs), in_sp...  71.9 us
    convert_element_type x8, local copies, waits for them, and re-layouts, scatter(): blocks.astype(jnp.bfloat16)  60.4 us
    pallas_call x1, Pallas kernels, attend_forward(): pl.pallas_call(attend_kernel, grid=(rows // LEN, cols, pairs), in_specs=[...  40.7 us
    psum x1, blocking collectives, per_device(): lax.psum(jnp.stack([gain_part_one, gain_part_two]), ('dp', 'col', 'row'))  39.6 us
    dot_general x1, matrix products, per_device(): up = jnp.einsum('td,cdn->ctn', normed_two, up_w, preferred_element_type=f32)  38.2 us
    all_gather x1, blocking collectives, per_device(): lax.all_gather(jnp.stack([gain_one, gain_two]), 'row', axis=1, tiled=True)  30.1 us
  transfers between devices with their start and end apart: 15, of which 11 were waited for; matrix products, arithmetic and copies ran while one was open for 17% of the time, Pallas kernels for 0%

profile of v1, /device:TPU:0, one launch (start us, length us, event | category | flops | bytes accessed | tf_op | source)
XLA Modules:
  0.0 1035.6 jit_solution(8785954474913134810)
XLA Ops:
  7.9 2.0 fusion.67
  13.4 4.2 all-to-all-start.2
  17.7 3.9 copy.83
  21.6 27.6 %all-to-all-done.2 = bf16[4,1024,256]{2,1,0:T(8,128)(2,1)S(1)} async-done(((bf16[4,1024,256]{2,1,0:T(8,128)(2,1)}), bf16[4,1024,256]{2,1,0:T(8,128)(2,1)S(1)}, u32[]{:S(2)}, u32[]{:S(2)}) %all-to-all-start.2) | async-done | bytes 2097184 | tf_op jit(solution)/shard_map/all_to_all | solution.py:192
  50.6 3.6 all-to-all-start
  54.3 30.1 %all_gather.24 = f32[2,1024]{1,0:T(2,128)S(1)} all-gather(f32[2,256]{1,0:T(2,128)S(1)} %pad_maximum_fusion.2), channel_id=1, replica_groups=mesh['dp'=2,'row'=4,'col'=4] {'row'}, dimensions={1}, use_global_device_ids=true | all-gather | bytes 10240 | tf_op jit(solution)/shard_map/all_gather | solution.py:183
  85.3 3.0 fusion.62
  88.3 4.0 bitcast_convert_fusion
  92.2 5.4 copy.94
  98.9 2.0 fusion.34
  100.9 3.2 copy.87
  104.1 1.8 copy.128
  106.0 19.2 %all-gather.14.cloned.1.call-done = bf16[4096,1,656]{0,2,1:T(8,128)(2,1)} async-done(((bf16[256,1,656]{0,2,1:T(8,128)(2,1)}), bf16[4096,1,656]{0,2,1:T(8,128)(2,1)}) %all-gather.14.cloned.1.call-update) | async-done | bytes 5373968 | tf_op jit(solution)/shard_map/all_gather | solution.py:166
  125.2 12.0 %reshape.159 = bf16[4,1024,656]{1,0,2:T(4,128)(2,1)} reshape(bf16[4096,1,656]{0,2,1:T(8,128)(2,1)} %all-gather.14.cloned.1.call-done) | data formatting | bytes 10747904 | tf_op jit(solution)/shard_map/reshape | solution.py:187
  137.2 48.4 %all-gather.16.cloned.1.call-done = bf16[4096,1,656]{0,2,1:T(8,128)(2,1)} async-done(((bf16[256,1,656]{0,2,1:T(8,128)(2,1)}), bf16[4096,1,656]{0,2,1:T(8,128)(2,1)}) %all-gather.16.cloned.1.call-update) | async-done | bytes 5373968 | tf_op jit(solution)/shard_map/all_gather | solution.py:166
  185.6 12.0 %reshape.160 = bf16[4,1024,656]{1,0,2:T(4,128)(2,1)} reshape(bf16[4096,1,656]{0,2,1:T(8,128)(2,1)} %all-gather.16.cloned.1.call-done) | data formatting | bytes 10747904 | tf_op jit(solution)/shard_map/reshape | solution.py:188
  197.6 45.0 %all-gather.18.cloned.1.call-done = bf16[10496,256]{1,0:T(8,128)(2,1)} async-done(((bf16[656,256]{1,0:T(8,128)(2,1)}), bf16[10496,256]{1,0:T(8,128)(2,1)}) %all-gather.18.cloned.1.call-update) | async-done | bytes 5373968 | tf_op jit(solution)/shard_map/all_gather | solution.py:166
  242.6 11.2 %fusion.59 = f32[4,656,1024,1]{2,1,3,0:T(8,128)} fusion(bf16[4,656,4,256]{3,1,2,0:T(8,128)(2,1)} %bitcast.270, bf16[4,1024,256]{2,1,0:T(8,128)(2,1)} %copy-done.6), kind=kOutput, calls=%fused_computation.86 | convolution fusion | flops 5502926848 | bytes 18219008 | tf_op jit(solution)/shard_map/td,cnd->ctn/dot_general | solution.py:210
  253.9 51.9 %all-gather.10.cloned.1.call-done = bf16[16,256,768]{2,1,0:T(8,128)(2,1)} async-done(((bf16[1,256,768]{2,1,0:T(8,128)(2,1)}), bf16[16,256,768]{2,1,0:T(8,128)(2,1)}) %all-gather.10.cloned.1.call-update) | async-done | bytes 6291472 | tf_op jit(solution)/shard_map/all_gather | solution.py:166
  305.8 12.4 %convolution_bitcast_fusion.q_ref.k_ref.v_ref = f32[4,1024,768]{2,1,0:T(8,128)} fusion(bf16[1024,1024,1]{0,1,2:T(8,128)(2,1)} %bitcast.275, bf16[4,1024,768]{2,1,0:T(8,128)(2,1)} %bitcast.301), kind=kOutput, calls=%fused_computation.46 | convolution fusion | flops 6442450944 | bytes 20971520 | tf_op jit(solution)/shard_map/td,cdn->ctn/dot_general | solution.py:199
  318.2 40.7 %attend_forward.1 = (bf16[1024,1024]{1,0:T(8,128)(2,1)}, bf16[1024,1024]{1,0:T(8,128)(2,1)}, bf16[1024,1024]{1,0:T(8,128)(2,1)}, bf16[1024,1024]{1,0:T(8,128)(2,1)}) custom-call(f32[4,1024,768]{2,1,0:T(8,128)} %convolution_bitcast_fusion.q_ref.k_ref.v_ref, f32[4,1024,768]{2,1,0:T(8,128)} %convolution_bitcast_fusion.q_ref.k_ref.v_ref, ...), custom_call_target="tpu_custom_call" | custom-call | tf_op jit(solution)/shard_map/attend_forward/pallas_call | solution.py:120
  358.9 4.5 fusion.64
  363.5 1.8 fusion.55
  365.3 11.1 %fusion.30 = f32[1024,4,656]{0,2,1:T(8,128)S(1)} fusion(bf16[1024,1024,1]{0,1,2:T(8,128)(2,1)} %fusion.55, bf16[4,1024,656]{1,0,2:T(4,128)(2,1)} %reshape.159), kind=kOutput, calls=%fused_computation.44 | convolution fusion | flops 5502926848 | bytes 18219008 | tf_op jit(solution)/shard_map/td,cdn->ctn/dot_general | solution.py:204
  376.5 38.2 %fusion.9 = (bf16[4,1024,656]{1,2,0:T(8,128)(2,1)}, f32[4,1024,656]{1,2,0:T(8,128)}, f32[1024,4,656]{0,2,1:T(8,128)}) fusion(f32[4,656,1024,1]{2,1,3,0:T(8,128)S(1)} %bitcast.265, f32[1024,4,656]{0,2,1:T(8,128)S(1)} %fusion.30, bf16[1024,1024,1]{0,1,2:T(8,128)(2,1)} %fusion.55, bf16[4,1024,656]{1,0,2:T(4,128)(2,1)} %reshape.160), kind=kOutput, calls=%fused_computation.19 | convolution fusion | flops 5699076096 | bytes 55836672 | tf_op jit(solution)/shard_map/td,cdn->ctn/dot_general | solution.py:205
  414.6 16.7 %fusion.1 = (bf16[4,1024,656]{1,2,0:T(8,128)(2,1)}, bf16[4,1024,656]{1,2,0:T(8,128)(2,1)}) fusion(f32[4,656,1024,1]{2,1,3,0:T(8,128)S(1)} %bitcast.265, f32[4,1024,656]{1,2,0:T(8,128)} %get-tuple-element.64, f32[1024,4,656]{0,2,1:T(8,128)} %copy-done.5, f32[1024,4,656]{0,2,1:T(8,128)} %get-tuple-element.82), kind=kLoop, calls=%fused_computation.4 | loop fusion | flops 16121856 | bytes 53739520 | tf_op jit(solution)/shard_map/convert_element_type | solution.py:215
  431.3 10.8 %fusion.24 = f32[1024,1024,1]{0,1,2:T(8,128)S(1)} fusion(bf16[4,1024,656]{1,2,0:T(8,128)(2,1)} %get-tuple-element.65, bf16[4,1024,656]{1,0,2:T(4,128)(2,1)} %reshape.160), kind=kOutput, calls=%fused_computation.38 | convolution fusion | flops 5502926848 | bytes 14942208 | tf_op jit(solution)/shard_map/ctn,cdn->td/dot_general | solution.py:222
  442.2 10.2 multiply_reduce_fusion
  452.4 3.5 fusion.65
  455.9 3.7 convolution_convert_fusion.do_ref
  459.6 71.9 %attend_backward.1 = (bf16[4,1024,256]{2,1,0:T(8,128)(2,1)}, bf16[4,1024,256]{2,1,0:T(8,128)(2,1)}, bf16[4,1024,256]{2,1,0:T(8,128)(2,1)}) custom-call(bf16[1024,1024]{1,0:T(8,128)(2,1)} %get-tuple-element.16.q_ref, bf16[1024,1024]{1,0:T(8,128)(2,1)} %get-tuple-element.17.k_ref, bf16[1024,1024]{1,0:T(8,128)(2,1)} %get-tuple-element.18.v_ref, ...), custom_call_target="tpu_custom_call" | custom-call | tf_op jit(solution)/shard_map/attend_backward/pallas_call | solution.py:138
  531.6 1.9 constant_dynamic-update-slice_fusion.2
  535.0 10.9 %fusion.47 = (f32[1024]{0:T(1024)S(1)}, f32[1024]{0:T(1024)S(1)}, f32[1024]{0:T(1024)S(1)}, bf16[1024,1024]{0,1:T(8,128)(2,1)S(1)}, f32[1024,1024,1]{0,1,2:T(8,128)}) fusion(bf16[4,1024,256]{1,2,0:T(8,128)(2,1)S(1)} %copy-done.1, f32[1024]{0:T(1024)S(1)} %copy-done.14, f32[1024]{0:T(1024)S(1)} %copy-done.16, f32[1024]{0:T(1024)S(1)} %bitcast.293, ...), kind=kOutput, calls=%fused_computation.67 | convolution fusion | flops 6453982208 | bytes 20996096 | tf_op jit(solution)/shard_map/ctn,cdn->td/dot_general | solution.py:235
  546.0 9.2 convert_bitcast_fusion
  555.1 8.6 copy.100
  563.8 5.9 convert_bitcast_fusion.3
  569.7 4.3 copy.103
  574.1 9.3 convert_bitcast_fusion.1
  583.4 6.5 copy.108
  589.9 10.5 %convert_element_type.150 = bf16[16,256,656]{1,0,2:T(8,128)(2,1)} reshape(bf16[4,1024,656]{1,0,2:T(4,128)(2,1)} %copy.108) | data formatting | bytes 10747904 | tf_op jit(solution)/shard_map/convert_element_type | solution.py:170
  600.4 6.8 copy.109
  607.3 9.1 convert_bitcast_fusion.2
  616.4 6.4 copy.105
  622.9 10.5 %convert_element_type.147 = bf16[16,256,656]{1,0,2:T(8,128)(2,1)} reshape(bf16[4,1024,656]{1,0,2:T(4,128)(2,1)} %copy.105) | data formatting | bytes 10747904 | tf_op jit(solution)/shard_map/convert_element_type | solution.py:170
  633.3 6.7 copy.106
  640.1 10.8 %fusion.50 = bf16[4,656,4,256]{3,1,2,0:T(8,128)(2,1)} fusion(bf16[4,1024,656]{1,2,0:T(8,128)(2,1)} %get-tuple-element.66, bf16[4,1024,256]{2,1,0:T(8,128)(2,1)} %copy-done.6), kind=kOutput, calls=%fused_computation.80 | convolution fusion | flops 5505613824 | bytes 12845056 | tf_op jit(solution)/shard_map/ctn,trd->crnd/dot_general | solution.py:211
  651.0 5.9 copy.127
  657.6 2.7 fusion.45
  660.3 3.6 all-to-all-start.3
  663.9 11.6 %fusion.48 = bf16[1024,1024]{0,1:T(8,128)(2,1)} fusion(f32[1024,1024]{0,1:T(8,128)} %copy-done.3, bf16[4,1024,656]{1,2,0:T(8,128)(2,1)} %get-tuple-element.66, bf16[4,656,1024]{2,1,0:T(8,128)(2,1)} %bitcast.273), kind=kOutput, calls=%fused_computation.72 | convolution fusion | flops 5505024000 | bytes 17039360 | tf_op jit(solution)/shard_map/ctn,cnd->td/dot_general | solution.py:207
  675.5 19.7 %all-to-all-done.3 = bf16[1024,4,256]{0,2,1:T(8,128)(2,1)S(1)} async-done(((bf16[1024,4,256]{0,2,1:T(8,128)(2,1)}), bf16[1024,4,256]{0,2,1:T(8,128)(2,1)S(1)}, u32[]{:S(2)}, u32[]{:S(2)}) %all-to-all-start.3) | async-done | bytes 2097184 | tf_op jit(solution)/shard_map/all_to_all | solution.py:242
  695.2 4.5 all-to-all-start.1
  699.8 1.9 copy.101
  701.7 18.2 %reduce-scatter.8.cloned.1.call-done = bf16[1,256,256]{2,1,0:T(8,128)(2,1)} async-done(((bf16[16,256,256]{2,1,0:T(8,128)(2,1)}), bf16[1,256,256]{2,1,0:T(8,128)(2,1)}) %reduce-scatter.8.cloned.1.call-update) | async-done | bytes 131088 | tf_op jit(solution)/shard_map/reduce_scatter | solution.py:170
  719.9 82.2 %reduce-scatter.12.cloned.1.call-done = bf16[1,256,656]{1,2,0:T(8,128)(2,1)} async-done(((bf16[16,256,656]{1,2,0:T(8,128)(2,1)}), bf16[1,256,656]{1,2,0:T(8,128)(2,1)}) %reduce-scatter.12.cloned.1.call-update) | async-done | bytes 335888 | tf_op jit(solution)/shard_map/reduce_scatter | solution.py:170
  802.1 82.4 %reduce-scatter.10.cloned.1.call-done = bf16[1,256,656]{1,2,0:T(8,128)(2,1)} async-done(((bf16[16,256,656]{1,2,0:T(8,128)(2,1)}), bf16[1,256,656]{1,2,0:T(8,128)(2,1)}) %reduce-scatter.10.cloned.1.call-update) | async-done | bytes 335888 | tf_op jit(solution)/shard_map/reduce_scatter | solution.py:170
  884.5 82.2 %reduce-scatter.14.cloned.1.call-done = bf16[1,656,256]{2,1,0:T(8,128)(2,1)} async-done(((bf16[16,656,256]{2,1,0:T(8,128)(2,1)}), bf16[1,656,256]{2,1,0:T(8,128)(2,1)}) %reduce-scatter.14.cloned.1.call-update) | async-done | bytes 335888 | tf_op jit(solution)/shard_map/reduce_scatter | solution.py:170
  966.7 39.6 %psum.47 = f32[2,1024]{1,0:T(2,128)S(1)} all-reduce(f32[2,1024]{1,0:T(2,128)S(1)} %pad_maximum_fusion.1), channel_id=1, replica_groups=mesh['dp'=2,'row'=4,'col'=4] {'dp','col','row'}, use_global_device_ids=true, to_apply=%region_20.0 | all-reduce | flops 2048 | bytes 16384 | tf_op jit(solution)/shard_map/psum | solution.py:246
  1007.0 2.5 copy.97
  1009.5 3.9 copy.93
  1013.5 7.3 all-reduce.3.cloned.1.call-done
  1020.8 2.0 copy.110
  1022.9 1.9 convert_element_type.154
  1026.4 2.2 maximum_convert_fusion
  (94 shorter events, 12.6 us)
Async XLA Ops:
  7.2 93.7 %all-gather.12.cloned.1.call-start = ((), (), s32[]{:S(2)}) async-start(), calls=%async_computation.15 | async-start | bytes 2228224 | tf_op jit(solution)/shard_map/all_gather | solution.py:166
  7.9 117.3 %all-gather.14.cloned.1.call-start = ((), (), s32[]{:S(2)}) async-start(), calls=%async_computation.16 | async-start | bytes 5709824 | tf_op jit(solution)/shard_map/all_gather | solution.py:166
  9.9 175.6 %all-gather.16.cloned.1.call-start = ((), (), s32[]{:S(2)}) async-start(), calls=%async_computation.17 | async-start | bytes 5709824 | tf_op jit(solution)/shard_map/all_gather | solution.py:166
  10.7 231.9 %all-gather.18.cloned.1.call-start = ((), (), s32[]{:S(2)}) async-start(), calls=%async_computation.18 | async-start | bytes 5709824 | tf_op jit(solution)/shard_map/all_gather | solution.py:166
  11.3 294.5 %all-gather.10.cloned.1.call-start = ((), (), s32[]{:S(2)}) async-start(), calls=%async_computation.9 | async-start | bytes 6684672 | tf_op jit(solution)/shard_map/all_gather | solution.py:166
  13.4 40.9 %copy-start.18 = (f32[256]{0:T(256)S(1)}, f32[256]{0:T(256)}, u32[]{:S(2)}) copy-start(f32[256]{0:T(256)} %param.10) | copy-start | bytes 3076
  13.4 40.9 %copy-start.19 = (f32[256]{0:T(256)S(1)}, f32[256]{0:T(256)}, u32[]{:S(2)}) copy-start(f32[256]{0:T(256)} %param.9) | copy-start | bytes 3076
  13.4 35.8 %all-to-all-start.2 = ((bf16[4,1024,256]{2,1,0:T(8,128)(2,1)}), bf16[4,1024,256]{2,1,0:T(8,128)(2,1)S(1)}, u32[]{:S(2)}, u32[]{:S(2)}) async-start(bf16[4,1024,256]{2,1,0:T(8,128)(2,1)} %bitcast.277), calls=%async_computation.2 | async-start | bytes 4194304 | tf_op jit(solution)/shard_map/all_to_all | solution.py:192
  49.2 1.4 copy-start.6
  50.6 47.0 %all-to-all-start = ((bf16[4,1024,256]{1,2,0:T(8,128)(2,1)}), bf16[4,1024,256]{1,2,0:T(8,128)(2,1)S(1)}, u32[]{:S(2)}, u32[]{:S(2)}) async-start(bf16[4,1024,256]{1,2,0:T(8,128)(2,1)} %copy.83), calls=%async_computation | async-start | bytes 4194304 | tf_op jit(solution)/shard_map/all_to_all | solution.py:182
  54.2 645.5 %reduce-scatter.6.cloned.1.call-start = ((), (), s32[]{:S(2)}) async-start(), calls=%async_computation.10 | async-start | bytes 6684672 | tf_op jit(solution)/shard_map/reduce_scatter | solution.py:170
  97.7 261.2 %copy-start = (bf16[4,1024,256]{1,2,0:T(8,128)(2,1)}, bf16[4,1024,256]{1,2,0:T(8,128)(2,1)S(1)}, u32[]{:S(2)}) copy-start(bf16[4,1024,256]{1,2,0:T(8,128)(2,1)S(1)} %all-to-all-done) | copy-start | bytes 6291460
  98.3 0.7 copy-start.13
  98.3 0.7 copy-start.15
  318.2 40.7 %copy-start.9 = (bf16[128,8,4,256]{3,1,2,0:T(8,128)(2,1)S(1)}, bf16[128,8,4,256]{3,1,2,0:T(8,128)(2,1)}, u32[]{:S(2)}) copy-start(bf16[128,8,4,256]{3,1,2,0:T(8,128)(2,1)} %copy.128) | copy-start | bytes 6291460
  363.4 88.9 %copy-start.3 = (f32[1024,1024]{0,1:T(8,128)}, f32[1024,1024]{0,1:T(8,128)S(1)}, u32[]{:S(2)}) copy-start(f32[1024,1024]{0,1:T(8,128)S(1)} %get-tuple-element.81) | copy-start | bytes 12582916
  363.5 13.0 %slice-start = ((s8[10747904]{0:T(1024)(128)(4,1)}), s8[4194304]{0:T(1024)(128)(4,1)S(1)}, s32[]{:S(2)}) async-start(s8[10747904]{0:T(1024)(128)(4,1)} %bitcast.264), calls=%async_computation.20 | async-start | bytes 8388608
  365.3 11.2 %slice-start.1 = ((s8[10747904]{0:T(1024)(128)(4,1)}), s8[4194304]{0:T(1024)(128)(4,1)S(1)}, s32[]{:S(2)}) async-start(s8[10747904]{0:T(1024)(128)(4,1)} %bitcast.264), calls=%async_computation.21 | async-start | bytes 8388608
  365.3 11.2 %slice-start.2 = ((s8[10747904]{0:T(1024)(128)(4,1)}), s8[2359296]{0:T(1024)(128)(4,1)S(1)}, s32[]{:S(2)}) async-start(s8[10747904]{0:T(1024)(128)(4,1)} %bitcast.264), calls=%async_computation.22 | async-start | bytes 4718592
  376.5 38.2 %copy-start.5 = (f32[1024,4,656]{0,2,1:T(8,128)}, f32[1024,4,656]{0,2,1:T(8,128)S(1)}, u32[]{:S(2)}) copy-start(f32[1024,4,656]{0,2,1:T(8,128)S(1)} %fusion.30) | copy-start | bytes 32243716
  431.3 10.8 %copy-start.20 = (bf16[4,1024,656]{1,2,0:T(8,128)(2,1)S(1)}, bf16[4,1024,656]{1,2,0:T(8,128)(2,1)}, u32[]{:S(2)}) copy-start(bf16[4,1024,656]{1,2,0:T(8,128)(2,1)} %get-tuple-element.63) | copy-start | bytes 16121860
  442.1 10.2 copy-start.4
  452.4 3.5 copy-start.10
  455.9 3.7 copy-start.8
  531.5 2.2 copy-start.12
  531.5 2.9 copy-start.11
  531.5 3.5 copy-start.1
  531.5 3.5 copy-start.14
  531.6 3.5 copy-start.16
  531.6 3.5 copy-start.17
  563.8 156.1 %reduce-scatter.8.cloned.1.call-start = ((), (), s32[]{:S(2)}) async-start(), calls=%async_computation.11 | async-start | bytes 2228224 | tf_op jit(solution)/shard_map/reduce_scatter | solution.py:170
  574.0 228.1 %reduce-scatter.12.cloned.1.call-start = ((), (), s32[]{:S(2)}) async-start(), calls=%async_computation.13 | async-start | bytes 5709824 | tf_op jit(solution)/shard_map/reduce_scatter | solution.py:170
  607.2 277.3 %reduce-scatter.10.cloned.1.call-start = ((), (), s32[]{:S(2)}) async-start(), calls=%async_computation.12 | async-start | bytes 5709824 | tf_op jit(solution)/shard_map/reduce_scatter | solution.py:170
  640.1 326.6 %reduce-scatter.14.cloned.1.call-start = ((), (), s32[]{:S(2)}) async-start(), calls=%async_computation.14 | async-start | bytes 5709824 | tf_op jit(solution)/shard_map/reduce_scatter | solution.py:170
  651.0 6.0 copy-start.2
  651.0 6.5 copy-start.7
  660.3 34.9 %all-to-all-start.3 = ((bf16[1024,4,256]{0,2,1:T(8,128)(2,1)}), bf16[1024,4,256]{0,2,1:T(8,128)(2,1)S(1)}, u32[]{:S(2)}, u32[]{:S(2)}) async-start(bf16[1024,4,256]{0,2,1:T(8,128)(2,1)} %bitcast.269), calls=%async_computation.3 | async-start | bytes 4194304 | tf_op jit(solution)/shard_map/all_to_all | solution.py:242
  695.2 314.3 %all-to-all-start.1 = ((bf16[1024,4,256]{0,2,1:T(8,128)(2,1)}), bf16[1024,4,256]{0,2,1:T(8,128)(2,1)}, u32[]{:S(2)}, u32[]{:S(2)}) async-start(bf16[1024,4,256]{0,2,1:T(8,128)(2,1)} %bitcast.279), calls=%async_computation.1 | async-start | bytes 4194304 | tf_op jit(solution)/shard_map/all_to_all | solution.py:208
  699.7 321.1 %all-reduce.3.cloned.1.call-start = ((), (), s32[]{:S(2)}) async-start(), calls=%async_computation.19 | async-start | bytes 3063808 | tf_op jit(solution)/shard_map/psum | solution.py:244
Sparse Core Ops, SparseCore 0:
  10.2 49.2 all-gather.11
  62.1 62.9 all-gather.13
  127.3 58.2 all-gather.15
  187.7 54.8 all-gather.17
  245.3 60.4 all-gather.9
  563.9 83.7 reduce-scatter.5
  652.0 67.8 reduce-scatter.7
  723.8 78.3 reduce-scatter.11
  806.0 78.4 reduce-scatter.9
  888.2 78.4 reduce-scatter.13
  969.9 50.8 all-reduce.2

commit v2 on v1

--- a/solution.py
+++ b/solution.py
@@ -167,7 +167,14 @@
 
 
 def scatter(blocks):
-    return lax.psum_scatter(blocks.astype(jnp.bfloat16), BOTH, scatter_dimension=0, tiled=False)
+    return lax.psum_scatter(blocks, BOTH, scatter_dimension=0, tiled=False)
+
+
+def sum_data(part):
+    if lax.axis_size("dp") == 2:
+        other = lax.ppermute(part, "dp", [(0, 1), (1, 0)])
+        return part.astype(jnp.float32) + other.astype(jnp.float32)
+    return lax.psum(part, "dp").astype(jnp.float32)
 
 
 def per_device(
@@ -179,17 +186,24 @@
     hid = w_down.shape[0]
     f32, bf16 = jnp.float32, jnp.bfloat16
 
+    first_pack = jnp.concatenate([query_key_value_weight.reshape(part, -1), w_out], axis=1)
+    first = gather(first_pack)
+    second_pack = jnp.concatenate(
+        [jnp.transpose(w_in, (1, 2, 0)), w_down[None]], axis=0
+    )
     residual_low = lax.all_to_all(layer_input, "row", 0, 1, tiled=True)
-    gains = lax.all_gather(jnp.stack([gain_one, gain_two]), "row", axis=1, tiled=True)
+    gains = jnp.broadcast_to(jnp.stack([gain_one, gain_two])[None], (rows_axis, 2, part))
+    gains = lax.all_to_all(gains, "row", 0, 0, tiled=True)
+    gains = jnp.swapaxes(gains, 0, 1).reshape(2, width)
     full_one, full_two = gains[0], gains[1]
-    qkv = gather(query_key_value_weight.reshape(part, -1)).reshape(cols, width, -1)
-    out = gather(w_out).reshape(cols, rows_axis, part, part)
-    gate_w = gather(w_in[:, 0]).reshape(cols, width, hid)
-    up_w = gather(w_in[:, 1]).reshape(cols, width, hid)
-    down = gather(w_down).reshape(cols, rows_axis, hid, part)
-    down = jnp.swapaxes(down, 1, 2).reshape(cols, hid, width)
+    first, second_pack = lax.optimization_barrier((first, second_pack))
+    second = gather(second_pack)
+    grad_out = lax.all_to_all(cotangent, "row", 0, 1, tiled=True)
+
+    first = first.reshape(cols, width, -1)
+    qkv = first[:, :, :-part]
+    out = first[:, :, -part:].reshape(cols, rows_axis, part, part)
     out = jnp.swapaxes(out, 1, 2).reshape(width, width)
-    grad_out = lax.all_to_all(cotangent, "row", 0, 1, tiled=True)
 
     residual_in = residual_low.astype(f32)
     rows = residual_in.shape[0]
@@ -201,57 +215,64 @@
     middle = residual_in + jnp.dot(mixed, out, preferred_element_type=f32)
     centred_two, rstd_two = norm_forward(middle)
     normed_two = (centred_two * full_two).astype(bf16)
-    gate = jnp.einsum("td,cdn->ctn", normed_two, gate_w, preferred_element_type=f32)
-    up = jnp.einsum("td,cdn->ctn", normed_two, up_w, preferred_element_type=f32)
+
+    second = second.reshape(cols, rows_axis, 3, hid, part)
+    second = jnp.transpose(second, (2, 0, 3, 1, 4)).reshape(3, cols * hid, width)
+    gate_w, up_w, down = second[0], second[1], second[2]
+    gate = dot(normed_two, gate_w, ((1,), (1,)))
+    up = dot(normed_two, up_w, ((1,), (1,)))
     hidden = (jax.nn.gelu(gate, approximate=False) * up).astype(bf16)
-    output = middle + jnp.einsum("ctn,cnd->td", hidden, down, preferred_element_type=f32)
+    output = middle + dot(hidden, down, ((1,), (0,)))
     output = lax.all_to_all(output.astype(bf16), "row", 1, 0, tiled=True)
 
-    grad_hidden = jnp.einsum("td,cnd->ctn", grad_out, down, preferred_element_type=f32)
-    grad_down = jnp.einsum("ctn,trd->crnd", hidden, grad_out.reshape(rows, rows_axis, part), preferred_element_type=f32)
-    grad_down = scatter(grad_down.reshape(-1, hid, part))
+    grad_hidden = dot(grad_out, down, ((1,), (1,)))
     _, pull = jax.vjp(lambda g, u: jax.nn.gelu(g, approximate=False) * u, gate, up)
     grad_gate, grad_up = pull(grad_hidden)
     grad_gate, grad_up = grad_gate.astype(bf16), grad_up.astype(bf16)
-    grad_gate_w = jnp.einsum("td,ctn->cdn", normed_two, grad_gate, preferred_element_type=f32)
-    grad_gate_w = scatter(grad_gate_w.reshape(-1, part, hid))
-    grad_up_w = jnp.einsum("td,ctn->cdn", normed_two, grad_up, preferred_element_type=f32)
-    grad_up_w = scatter(grad_up_w.reshape(-1, part, hid))
-    grad_normed_two = jnp.einsum(
-        "ctn,cdn->td", grad_gate, gate_w, preferred_element_type=f32
-    ) + jnp.einsum("ctn,cdn->td", grad_up, up_w, preferred_element_type=f32)
+
+    def blocks(grad):
+        grad = grad.astype(bf16).reshape(cols, hid, rows_axis, part)
+        return jnp.swapaxes(grad, 1, 2).reshape(-1, hid, part)
+
+    grad_second = jnp.stack(
+        [
+            blocks(dot(grad_gate, normed_two, ((0,), (0,)))),
+            blocks(dot(grad_up, normed_two, ((0,), (0,)))),
+            blocks(dot(hidden, grad_out, ((0,), (0,)))),
+        ],
+        axis=1,
+    )
+    grad_second = scatter(grad_second)
+    grad_normed_two = dot(grad_gate, gate_w, ((1,), (0,))) + dot(grad_up, up_w, ((1,), (0,)))
     grad_norm_two, gain_part_two = norm_backward(grad_normed_two, centred_two, rstd_two, full_two)
     grad_middle = grad_out.astype(f32) + grad_norm_two
     branch = grad_middle.astype(bf16)
     grad_mixed = dot(branch, out, ((1,), (1,))).astype(bf16)
-    grad_w_out = jnp.einsum(
-        "tcm,trd->crmd",
-        mixed.reshape(rows, cols, part),
-        branch.reshape(rows, rows_axis, part),
-        preferred_element_type=f32,
-    )
-    grad_w_out = scatter(grad_w_out.reshape(-1, part, part))
+    grad_w_out = dot(mixed, branch, ((0,), (0,))).astype(bf16)
+    grad_w_out = grad_w_out.reshape(cols, part, rows_axis, part)
+    grad_w_out = jnp.swapaxes(grad_w_out, 1, 2).reshape(-1, part, part)
     grad_projected = attend_backward(query, key, value, grad_mixed, cosine, sine, cols)
+    grad_qkv = jnp.einsum("td,ctn->cdn", normed_one, grad_projected, preferred_element_type=f32)
+    grad_qkv = grad_qkv.astype(bf16).reshape(cols * rows_axis, part, -1)
+    grad_first = scatter(jnp.concatenate([grad_qkv, grad_w_out], axis=2))
     grad_normed_one = jnp.einsum("ctn,cdn->td", grad_projected, qkv, preferred_element_type=f32)
-    grad_qkv = jnp.einsum("td,ctn->cdn", normed_one, grad_projected, preferred_element_type=f32)
-    grad_qkv = scatter(grad_qkv.reshape(-1, part, qkv.shape[2]))
     grad_norm_one, gain_part_one = norm_backward(
         grad_normed_one, centred_one, rstd_one, full_one
     )
     grad_input = (grad_middle + grad_norm_one).astype(bf16)
     grad_input = lax.all_to_all(grad_input, "row", 1, 0, tiled=True)
 
-    sums = lax.psum((grad_down, grad_gate_w, grad_up_w, grad_w_out, grad_qkv), "dp")
-    grad_down, grad_gate_w, grad_up_w, grad_w_out, grad_qkv = (s.astype(f32) for s in sums)
+    grad_second = sum_data(grad_second)
+    grad_first = sum_data(grad_first)
     gain_sums = lax.psum(jnp.stack([gain_part_one, gain_part_two]), ("dp", "col", "row"))
     mine = lax.dynamic_slice_in_dim(gain_sums, lax.axis_index("row") * part, part, 1)
     return (
         output,
         grad_input,
-        grad_qkv.reshape(query_key_value_weight.shape),
-        grad_w_out,
-        jnp.stack([grad_gate_w, grad_up_w], axis=1),
-        grad_down,
+        grad_first[:, :-part].reshape(query_key_value_weight.shape),
+        grad_first[:, -part:],
+        jnp.transpose(grad_second[:2], (2, 0, 1)),
+        grad_second[2],
         mine[0],
         mine[1],
     )

time: 1050 us -> 807 us (0.77)
  waiting for transfers between devices: 486 us -> 224 us
  local copies, waits for them, and re-layouts: 127 us -> 174 us
  blocking collectives: 69.7 us -> 45.7 us
    reduce_scatter x5 -> x2, waiting for transfers between devices: 265 us -> 87 us  [scatter(): return lax.psum_scatter(blocks, BOTH, scatter_dimension=0, tiled=False)]
    dot_general x1 -> x11, matrix products: 3.72 us -> 138 us  [dot(): lax.dot_general(left, right, (over, ((), ())), preferred_element_type=jnp...]
    dot_general x10 -> x0, matrix products: 128 us -> none  [the longest x1 38.2 us: per_device(): up = jnp.einsum('td,cdn->ctn', normed_two, up_w, preferred_element_type=f32)]
    all_gather x5 -> x2, waiting for transfers between devices: 165 us -> 96.8 us  [gather(): return lax.all_gather(block, BOTH, axis=0, tiled=False)]
    convert_element_type x9 -> x1, local copies, waits for them, and re-layouts: 65.8 us -> 8.91 us  [per_device(): grad_qkv = grad_qkv.astype(bf16).reshape(cols * rows_axis, part, -1)]
    reshape x4 -> x6, local copies, waits for them, and re-layouts: 33.2 us -> 71.3 us  [the longest x1 33.8 us: per_device(): second = second.reshape(cols, rows_axis, 3, hid, part)]
    all_gather x1 -> x0, blocking collectives: 30.1 us -> none  [per_device(): lax.all_gather(jnp.stack([gain_one, gain_two]), 'row', axis=1, tiled=True)]
    unnamed x53 -> x92, local copies, waits for them, and re-layouts: 11 us -> 38.8 us
  transfers between devices with their start and end apart: 15 -> 11, of which waited for: 11 -> 6; matrix products, arithmetic and copies ran while one was open for 17% -> 27% of each run, Pallas kernels for 0% -> 14%
where the time goes in v2:
time: 807 us; the launch traced here: 800 us
  waiting for transfers between devices  224 us (28%)
  local copies, waits for them, and re-layouts  174 us (22%)
  matrix products  173 us (21%)
  Pallas kernels  112 us (14%)
  blocking collectives  45.7 us (6%)
  other arithmetic  33.9 us (4%)
  starting transfers between devices  22.5 us (3%)
  between operations  14.6 us (2%)
    dot_general x11, matrix products, dot(): lax.dot_general(left, right, (over, ((), ())), preferred_element_type=jnp...  138 us
    all_gather x2, waiting for transfers between devices, gather(): return lax.all_gather(block, BOTH, axis=0, tiled=False)  96.8 us
    reduce_scatter x2, waiting for transfers between devices, scatter(): return lax.psum_scatter(blocks, BOTH, scatter_dimension=0, tiled=False)  87 us
    pallas_call x1, Pallas kernels, attend_backward(): pl.pallas_call(attend_back_kernel, grid=(rows // LEN, cols, pairs), in_sp...  71.7 us
    psum x1, blocking collectives, per_device(): lax.psum(jnp.stack([gain_part_one, gain_part_two]), ('dp', 'col', 'row'))  45.7 us
    pallas_call x1, Pallas kernels, attend_forward(): pl.pallas_call(attend_kernel, grid=(rows // LEN, cols, pairs), in_specs=[...  40.7 us
    unnamed x92, local copies, waits for them, and re-layouts  38.8 us
    reshape x1, local copies, waits for them, and re-layouts, per_device(): second = second.reshape(cols, rows_axis, 3, hid, part)  33.8 us
  transfers between devices with their start and end apart: 11, of which 6 were waited for; matrix products, arithmetic and copies ran while one was open for 27% of the time, Pallas kernels for 14%

profile of v2, /device:TPU:0, one launch (start us, length us, event | category | flops | bytes accessed | tf_op | source)
XLA Modules:
  0.0 800.2 jit_solution(5256022043707196001)
XLA Ops:
  10.3 2.2 pad_maximum_fusion.2
  12.5 79.0 %all-gather.5.cloned.1.call-done = bf16[4096,1024]{0,1:T(8,128)(2,1)} async-done(((bf16[256,1024]{0,1:T(8,128)(2,1)}), bf16[4096,1024]{0,1:T(8,128)(2,1)}) %all-gather.5.cloned.1.call-update) | async-done | bytes 8388624 | tf_op jit(solution)/shard_map/all_gather | solution.py:166
  91.6 9.9 %copy.81 = bf16[128,8,16,256]{3,2,1,0:T(8,128)(2,1)} copy(bf16[128,8,16,256]{3,1,2,0:T(8,128)(2,1)} %bitcast.162) | data formatting | bytes 16777216
  102.1 3.2 all-to-all-start.1
  105.4 2.4 copy.51
  109.1 3.6 all-to-all-start
  112.7 4.0 copy.61
  117.0 3.0 fusion.31
  120.0 24.1 %all-to-all-done = bf16[4,1024,256]{1,2,0:T(8,128)(2,1)S(1)} async-done(((bf16[4,1024,256]{1,2,0:T(8,128)(2,1)}), bf16[4,1024,256]{1,2,0:T(8,128)(2,1)S(1)}, u32[]{:S(2)}, u32[]{:S(2)}) %all-to-all-start) | async-done | bytes 2097184 | tf_op jit(solution)/shard_map/all_to_all | solution.py:194
  144.1 4.4 all-to-all-start.3
  149.9 2.0 fusion.20
  151.9 12.2 %copy.54 = bf16[16,256,1024]{2,1,0:T(8,128)(2,1)} copy(bf16[16,256,1024]{1,0,2:T(8,128)(2,1)} %bitcast.145) | data formatting | bytes 16777216 | tf_op jit(solution)/shard_map/optimization_barrier | solution.py:199
  164.1 1.9 slice.59
  166.0 1.6 copy.58
  168.7 9.8 %fusion.11.q_ref.k_ref.v_ref = f32[4,1024,768]{2,1,0:T(8,128)} fusion(bf16[4,1024,1024]{2,1,0:T(8,128)(2,1)S(1)} %bitcast.161, bf16[1024,1024]{0,1:T(8,128)(2,1)S(1)} %copy-done.10), kind=kOutput, calls=%fused_computation.32 | convolution fusion | flops 6442450944 | bytes 20971520 | tf_op jit(solution)/shard_map/td,cdn->ctn/dot_general | solution.py:213
  178.5 40.7 %attend_forward.1 = (bf16[1024,1024]{1,0:T(8,128)(2,1)}, bf16[1024,1024]{1,0:T(8,128)(2,1)}, bf16[1024,1024]{1,0:T(8,128)(2,1)}, bf16[1024,1024]{1,0:T(8,128)(2,1)}) custom-call(f32[4,1024,768]{2,1,0:T(8,128)} %fusion.11.q_ref.k_ref.v_ref, f32[4,1024,768]{2,1,0:T(8,128)} %fusion.11.q_ref.k_ref.v_ref, f32[4,1024,768]{2,1,0:T(8,128)} %fusion.11.q_ref.k_ref.v_ref, ...), custom_call_target="tpu_custom_call" | custom-call | tf_op jit(solution)/shard_map/attend_forward/pallas_call | solution.py:120
  219.3 4.4 fusion.33
  223.7 1.9 copy-done.6
  225.6 1.8 multiply_convert_fusion.1
  227.5 17.8 %all-gather.7.cloned.1.call-done = bf16[48,656,256]{2,1,0:T(8,128)(2,1)} async-done(((bf16[3,656,256]{2,1,0:T(8,128)(2,1)}), bf16[48,656,256]{2,1,0:T(8,128)(2,1)}) %all-gather.7.cloned.1.call-update) | async-done | bytes 16121872 | tf_op jit(solution)/shard_map/all_gather | solution.py:166
  245.3 33.8 %copy.87 = bf16[4,4,3,656,256]{4,1,3,0,2:T(4,128)(2,1)S(1)} copy(bf16[4,4,3,656,256]{4,3,2,1,0:T(8,128)(2,1)} %bitcast.158) | data formatting | bytes 32243712 | tf_op jit(solution)/shard_map/reshape | solution.py:219
  279.0 7.4 fusion.35
  286.4 4.5 copy.83
  291.0 4.1 copy.85
  295.1 4.1 copy.84
  299.2 8.8 %fusion.39 = f32[1024,2624]{0,1:T(8,128)} fusion(bf16[2624,1024]{1,0:T(8,128)(2,1)S(1)} %bitcast.173, bf16[1024,1024]{0,1:T(8,128)(2,1)S(1)} %copy-done.15), kind=kOutput, calls=%fused_computation.98 | convolution fusion | flops 5502926848 | bytes 18219008 | tf_op jit(solution)/shard_map/dot_general | solution.py:47
  308.0 32.4 %fusion.1 = (bf16[1024,2624]{0,1:T(8,128)(2,1)}, f32[1024,2624]{0,1:T(8,128)}, f32[2624,1024]{1,0:T(8,128)}) fusion(f32[1024,2624]{0,1:T(8,128)} %fusion.39, bf16[2624,1024]{1,0:T(8,128)(2,1)} %bitcast.169, bf16[1024,1024]{0,1:T(8,128)(2,1)} %bitcast.24), kind=kOutput, calls=%fused_computation.6 | convolution fusion | flops 5680267264 | bytes 45088768 | tf_op jit(solution)/shard_map/dot_general | solution.py:47
  340.5 23.5 %add_convert_fusion = (bf16[1024,2624]{0,1:T(8,128)(2,1)}, bf16[1024,2624]{0,1:T(8,128)(2,1)}) fusion(f32[1024,2624]{0,1:T(8,128)} %get-tuple-element.53, f32[2624,1024]{1,0:T(8,128)} %get-tuple-element.70, f32[1024,2624]{0,1:T(8,128)} %fusion.39, bf16[2624,1024]{1,0:T(8,128)(2,1)} %bitcast.171, bf16[1024,1024]{0,1:T(8,128)(2,1)S(1)} %copy-done.16), kind=kOutput, calls=%fused_computation.7 | convolution fusion | flops 5551292416 | bytes 50462720 | tf_op jit(solution)/shard_map/dot_general | solution.py:47
  364.0 10.1 %convolution_convert_fusion.2 = bf16[2624,1024]{1,0:T(8,128)(2,1)} fusion(bf16[1024,2624]{0,1:T(8,128)(2,1)} %get-tuple-element.54, bf16[1024,1024]{0,1:T(8,128)(2,1)S(1)} %copy-done.16), kind=kOutput, calls=%fused_computation.27 | convolution fusion | flops 5505613824 | bytes 12845056 | tf_op jit(solution)/shard_map/dot_general | solution.py:47
  374.1 10.8 %reshape.151 = bf16[4,656,4,256]{3,2,1,0:T(4,128)(2,1)} reshape(bf16[2624,1024]{1,0:T(8,128)(2,1)} %convolution_convert_fusion.2) | data formatting | bytes 10747904 | tf_op jit(solution)/shard_map/reshape | solution.py:234
  384.9 5.6 copy.69
  390.5 10.4 %convolution_convert_fusion.1 = bf16[2624,1024]{1,0:T(8,128)(2,1)} fusion(bf16[1024,2624]{0,1:T(8,128)(2,1)} %get-tuple-element.52, bf16[1024,1024]{0,1:T(8,128)(2,1)S(1)} %copy-done.16), kind=kOutput, calls=%fused_computation.26 | convolution fusion | flops 5505613824 | bytes 12845056 | tf_op jit(solution)/shard_map/dot_general | solution.py:47
  400.8 10.9 %reshape.152 = bf16[4,656,4,256]{3,2,1,0:T(4,128)(2,1)} reshape(bf16[2624,1024]{1,0:T(8,128)(2,1)} %convolution_convert_fusion.1) | data formatting | bytes 10747904 | tf_op jit(solution)/shard_map/reshape | solution.py:234
  411.7 5.8 copy.70
  417.5 9.1 %convolution_convert_fusion = bf16[2624,1024]{1,0:T(8,128)(2,1)} fusion(bf16[1024,2624]{0,1:T(8,128)(2,1)S(1)} %bitcast.202, bf16[1024,1024]{0,1:T(8,128)(2,1)} %bitcast.24), kind=kOutput, calls=%fused_computation.25 | convolution fusion | flops 5505613824 | bytes 12845056 | tf_op jit(solution)/shard_map/dot_general | solution.py:47
  426.6 10.9 %reshape.153 = bf16[4,656,4,256]{3,2,1,0:T(4,128)(2,1)} reshape(bf16[2624,1024]{1,0:T(8,128)(2,1)} %convolution_convert_fusion) | data formatting | bytes 10747904 | tf_op jit(solution)/shard_map/reshape | solution.py:234
  437.5 3.4 copy.71
  441.3 1.6 copy-done.2
  442.9 6.8 pad_maximum_fusion
  449.8 10.7 %fusion.38 = f32[1024,1024]{0,1:T(8,128)S(1)} fusion(bf16[1024,2624]{0,1:T(8,128)(2,1)} %get-tuple-element.54, bf16[2624,1024]{1,0:T(8,128)(2,1)} %bitcast.174), kind=kOutput, calls=%fused_computation.97 | convolution fusion | flops 5502926848 | bytes 14942208 | tf_op jit(solution)/shard_map/dot_general | solution.py:47
  460.5 12.1 %multiply_reduce_fusion = (f32[1024]{0:T(1024)S(1)}, f32[1024]{0:T(1024)S(1)}, f32[1024]{0:T(1024)S(1)}, f32[1024,1024]{0,1:T(8,128)S(1)}) fusion(f32[1024,1024]{0,1:T(8,128)S(1)} %copy-done.7, f32[1024]{0:T(1024)S(1)} %copy-done.33, f32[1024]{0:T(1024)S(1)} %copy-done.31, f32[1024]{0:T(1024)S(1)} %bitcast.192, f32[1024,1024]{0,1:T(8,128)S(1)} %fusion.38, ...), kind=kOutput, calls=%fused_computation.51 | convolution fusion | flops 5512360960 | bytes 23355392 | tf_op jit(solution)/shard_map/dot_general | solution.py:47
  472.7 3.3 multiply_add_fusion
  476.0 3.7 convolution_convert_fusion.4.do_ref
  479.8 71.7 %attend_backward.1 = (bf16[4,1024,256]{2,1,0:T(8,128)(2,1)}, bf16[4,1024,256]{2,1,0:T(8,128)(2,1)}, bf16[4,1024,256]{2,1,0:T(8,128)(2,1)}) custom-call(bf16[1024,1024]{1,0:T(8,128)(2,1)} %get-tuple-element.20.q_ref, bf16[1024,1024]{1,0:T(8,128)(2,1)} %get-tuple-element.21.k_ref, bf16[1024,1024]{1,0:T(8,128)(2,1)} %get-tuple-element.22.v_ref, ...), custom_call_target="tpu_custom_call" | custom-call | tf_op jit(solution)/shard_map/attend_backward/pallas_call | solution.py:138
  551.5 1.9 constant_dynamic-update-slice_fusion.2
  554.5 2.7 copy-done.20
  557.2 9.1 %convert_bitcast_fusion = bf16[4,1024,768]{1,2,0:T(8,128)(2,1)} fusion(bf16[4,1024,768]{2,1,0:T(8,128)(2,1)S(1)} %constant_dynamic-update-slice_fusion, bf16[1024,1024]{0,1:T(8,128)(2,1)S(1)} %copy-done.11), kind=kOutput, calls=%fused_computation.24 | convolution fusion | flops 6445596672 | bytes 14680064 | tf_op jit(solution)/shard_map/td,ctn->cdn/dot_general | solution.py:255
  566.3 8.9 %copy.66 = bf16[4,1024,768]{2,1,0:T(8,128)(2,1)} copy(bf16[4,1024,768]{1,2,0:T(8,128)(2,1)} %convert_bitcast_fusion) | data formatting | bytes 12582912 | tf_op jit(solution)/shard_map/convert_element_type | solution.py:256
  575.2 6.0 convolution_convert_fusion.3
  581.2 3.4 reshape.148
  584.6 1.7 copy.67
  586.3 7.8 pad_maximum_fusion.1
  594.2 1.6 copy-done.1
  595.7 11.6 %fusion.14 = (f32[1024]{0:T(1024)S(1)}, f32[1024]{0:T(1024)S(1)}, f32[1024]{0:T(1024)S(1)}, f32[1024,1024,1]{0,1,2:T(8,128)S(1)}) fusion(bf16[4,1024,256]{1,2,0:T(8,128)(2,1)S(1)} %copy-done.1, f32[1024]{0:T(1024)S(1)} %copy-done.27, f32[1024]{0:T(1024)S(1)} %copy-done.25, f32[1024]{0:T(1024)S(1)} %bitcast.189, bf16[4,1024,768]{2,1,0:T(8,128)(2,1)} %copy-done.20, ...), kind=kOutput, calls=%fused_computation.35 | convolution fusion | flops 6451885056 | bytes 18898944 | tf_op jit(solution)/shard_map/ctn,cdn->td/dot_general | solution.py:258
  607.3 2.7 fusion.25
  610.0 3.6 all-to-all-start.4
  613.6 11.4 %add_convert_fusion.1 = bf16[1024,1024]{0,1:T(8,128)(2,1)} fusion(f32[1024,1024]{0,1:T(8,128)} %copy-done.6, bf16[1024,2624]{0,1:T(8,128)(2,1)} %get-tuple-element.55, bf16[2624,1024]{1,0:T(8,128)(2,1)} %bitcast.170), kind=kOutput, calls=%fused_computation.54 | convolution fusion | flops 5505024000 | bytes 17039360 | tf_op jit(solution)/shard_map/dot_general | solution.py:47
  625.0 14.3 %all-to-all-done.4 = bf16[1024,4,256]{0,2,1:T(8,128)(2,1)S(1)} async-done(((bf16[1024,4,256]{0,2,1:T(8,128)(2,1)}), bf16[1024,4,256]{0,2,1:T(8,128)(2,1)S(1)}, u32[]{:S(2)}, u32[]{:S(2)}) %all-to-all-start.4) | async-done | bytes 2097184 | tf_op jit(solution)/shard_map/all_to_all | solution.py:263
  639.3 4.5 all-to-all-start.2
  645.1 87.0 %reduce-scatter.3.cloned.1.call-done = bf16[1,256,1024]{2,1,0:T(8,128)(2,1)} async-done(((bf16[16,256,1024]{2,1,0:T(8,128)(2,1)}), bf16[1,256,1024]{2,1,0:T(8,128)(2,1)}) %reduce-scatter.3.cloned.1.call-update) | async-done | bytes 524304 | tf_op jit(solution)/shard_map/reduce_scatter | solution.py:170
  732.1 1.4 collective-permute-start
  733.6 45.7 %psum.7 = f32[2,1024]{1,0:T(2,128)S(1)} all-reduce(f32[2,1024]{1,0:T(2,128)S(1)} %pad_maximum_fusion.5), channel_id=1, replica_groups=mesh['dp'=2,'row'=4,'col'=4] {'dp','col','row'}, use_global_device_ids=true, to_apply=%region_12.0 | all-reduce | flops 2048 | bytes 16384 | tf_op jit(solution)/shard_map/psum | solution.py:267
  779.9 2.5 copy.63
  782.4 4.0 copy.60
  (123 shorter events, 18.4 us)
Async XLA Ops:
  7.2 84.4 %all-gather.5.cloned.1.call-start = ((), (), s32[]{:S(2)}) async-start(), calls=%async_computation.9 | async-start | bytes 8912896 | tf_op jit(solution)/shard_map/all_gather | solution.py:166
  10.2 235.0 %all-gather.7.cloned.1.call-start = ((), (), s32[]{:S(2)}) async-start(), calls=%async_computation.10 | async-start | bytes 17129472 | tf_op jit(solution)/shard_map/all_gather | solution.py:166
  91.6 9.9 %copy-start.34 = (f32[256]{0:T(256)S(1)}, f32[256]{0:T(256)}, u32[]{:S(2)}) copy-start(f32[256]{0:T(256)} %param.10) | copy-start | bytes 3076
  91.6 9.9 %copy-start.35 = (f32[256]{0:T(256)S(1)}, f32[256]{0:T(256)}, u32[]{:S(2)}) copy-start(f32[256]{0:T(256)} %param.9) | copy-start | bytes 3076
  91.6 13.8 %copy-start.12 = (bf16[4096,256]{1,0:T(8,128)(2,1)S(1)}, bf16[4096,256]{1,0:T(8,128)(2,1)}, u32[]{:S(2)}) copy-start(bf16[4096,256]{1,0:T(8,128)(2,1)} %param.8) | copy-start | bytes 6291460
  102.1 7.0 all-to-all-start.1
  109.1 34.9 %all-to-all-start = ((bf16[4,1024,256]{1,2,0:T(8,128)(2,1)}), bf16[4,1024,256]{1,2,0:T(8,128)(2,1)S(1)}, u32[]{:S(2)}, u32[]{:S(2)}) async-start(bf16[4,1024,256]{1,2,0:T(8,128)(2,1)} %copy.51), calls=%async_computation | async-start | bytes 4194304 | tf_op jit(solution)/shard_map/all_to_all | solution.py:194
  120.0 44.1 %copy-start.22 = (f32[1,4,256]{2,0,1:T(1,128)}, f32[1,4,256]{2,0,1:T(1,128)S(1)}, u32[]{:S(2)}) copy-start(f32[1,4,256]{2,0,1:T(1,128)S(1)} %get-tuple-element.64) | copy-start | bytes 12292
  120.0 103.7 %copy-start.28 = (f32[1,4,256]{2,0,1:T(1,128)}, f32[1,4,256]{2,0,1:T(1,128)S(1)}, u32[]{:S(2)}) copy-start(f32[1,4,256]{2,0,1:T(1,128)S(1)} %get-tuple-element.63) | copy-start | bytes 12292
  144.1 75.2 %copy-start = (bf16[4,1024,256]{1,2,0:T(8,128)(2,1)}, bf16[4,1024,256]{1,2,0:T(8,128)(2,1)S(1)}, u32[]{:S(2)}) copy-start(bf16[4,1024,256]{1,2,0:T(8,128)(2,1)S(1)} %all-to-all-done) | copy-start | bytes 6291460
  144.1 163.9 %all-to-all-start.3 = ((bf16[4,1024,256]{1,2,0:T(8,128)(2,1)}), bf16[4,1024,256]{1,2,0:T(8,128)(2,1)}, u32[]{:S(2)}, u32[]{:S(2)}) async-start(bf16[4,1024,256]{1,2,0:T(8,128)(2,1)} %copy.61), calls=%async_computation.3 | async-start | bytes 4194304 | tf_op jit(solution)/shard_map/all_to_all | solution.py:201
  148.5 495.3 %reduce-scatter.5.cloned.1.call-start = ((), (), s32[]{:S(2)}) async-start(), calls=%async_computation.8 | async-start | bytes 17129472 | tf_op jit(solution)/shard_map/reduce_scatter | solution.py:170
  149.3 0.6 copy-start.24
  149.3 0.6 copy-start.26
  164.1 4.0 copy-start.8
  164.1 4.6 copy-start.10
  168.7 50.5 %copy-start.13 = (bf16[128,8,4,256]{3,1,2,0:T(8,128)(2,1)}, bf16[128,8,4,256]{3,1,2,0:T(8,128)(2,1)S(1)}, u32[]{:S(2)}) copy-start(bf16[128,8,4,256]{3,1,2,0:T(8,128)(2,1)S(1)} %copy.82) | copy-start | bytes 6291460
  223.6 2.0 copy-start.6
  223.7 2.0 copy-start.30
  223.7 2.0 copy-start.32
  286.4 4.5 copy-start.3
  290.9 8.2 %copy-start.9 = (bf16[328,8,4,256]{3,1,2,0:T(8,128)(2,1)}, bf16[328,8,4,256]{3,1,2,0:T(8,128)(2,1)S(1)}, u32[]{:S(2)}) copy-start(bf16[328,8,4,256]{3,1,2,0:T(8,128)(2,1)S(1)} %copy.83) | copy-start | bytes 16121860
  295.1 4.1 copy-start.15
  308.0 32.4 %copy-start.16 = (bf16[1024,1024]{0,1:T(8,128)(2,1)S(1)}, bf16[1024,1024]{0,1:T(8,128)(2,1)}, u32[]{:S(2)}) copy-start(bf16[1024,1024]{0,1:T(8,128)(2,1)} %multiply_convert_fusion.1) | copy-start | bytes 6291460
  400.8 16.7 %slice-start.2 = ((s8[5373952]{0:T(1024)(128)(4,1)}), s8[1179648]{0:T(1024)(128)(4,1)S(1)}, s32[]{:S(2)}) async-start(s8[5373952]{0:T(1024)(128)(4,1)} %bitcast.201), calls=%async_computation.13 | async-start | bytes 2359296
  411.7 5.8 slice-start.3
  426.6 14.3 %slice-start = ((s8[5373952]{0:T(1024)(128)(4,1)}), s8[1179648]{0:T(1024)(128)(4,1)S(1)}, s32[]{:S(2)}) async-start(s8[5373952]{0:T(1024)(128)(4,1)} %bitcast.150), calls=%async_computation.11 | async-start | bytes 2359296
  437.5 3.8 slice-start.1
  437.5 5.4 copy-start.2
  449.7 10.8 %copy-start.29 = (f32[1,4,256]{2,0,1:T(1,128)S(1)}, f32[1,4,256]{2,0,1:T(1,128)}, u32[]{:S(2)}) copy-start(f32[1,4,256]{2,0,1:T(1,128)} %copy-done.28) | copy-start | bytes 12292
  449.7 10.8 %copy-start.31 = (f32[1024]{0:T(1024)S(1)}, f32[1024]{0:T(1024)}, u32[]{:S(2)}) copy-start(f32[1024]{0:T(1024)} %copy-done.30) | copy-start | bytes 12292
  449.7 10.8 %copy-start.33 = (f32[1024]{0:T(1024)S(1)}, f32[1024]{0:T(1024)}, u32[]{:S(2)}) copy-start(f32[1024]{0:T(1024)} %copy-done.32) | copy-start | bytes 12292
  449.7 282.4 %reduce-scatter.3.cloned.1.call-start = ((), (), s32[]{:S(2)}) async-start(), calls=%async_computation.7 | async-start | bytes 8912896 | tf_op jit(solution)/shard_map/reduce_scatter | solution.py:170
  449.8 10.7 %copy-start.7 = (f32[1024,1024]{0,1:T(8,128)S(1)}, f32[1024,1024]{0,1:T(8,128)}, u32[]{:S(2)}) copy-start(f32[1024,1024]{0,1:T(8,128)} %copy-done.6) | copy-start | bytes 12582916
  472.7 3.3 copy-start.14
  476.0 3.7 copy-start.4
  551.5 2.2 copy-start.18
  551.5 2.9 copy-start.17
  551.5 5.8 copy-start.11
  554.5 2.7 copy-start.20
  566.3 8.9 %copy-start.36 = (bf16[1024,1024]{1,0:T(8,128)(2,1)S(1)}, bf16[1024,1024]{1,0:T(8,128)(2,1)}, u32[]{:S(2)}) copy-start(bf16[1024,1024]{1,0:T(8,128)(2,1)} %get-tuple-element.18) | copy-start | bytes 6291460
  594.1 1.6 copy-start.1
  594.1 1.6 copy-start.23
  594.1 1.6 copy-start.25
  594.1 1.6 copy-start.27
  595.7 11.6 %copy-start.5 = (f32[1024,1024]{0,1:T(8,128)S(1)}, f32[1024,1024]{0,1:T(8,128)}, u32[]{:S(2)}) copy-start(f32[1024,1024]{0,1:T(8,128)} %copy-done.4) | copy-start | bytes 12582916
  610.0 29.3 %all-to-all-start.4 = ((bf16[1024,4,256]{0,2,1:T(8,128)(2,1)}), bf16[1024,4,256]{0,2,1:T(8,128)(2,1)S(1)}, u32[]{:S(2)}, u32[]{:S(2)}) async-start(bf16[1024,4,256]{0,2,1:T(8,128)(2,1)} %bitcast.167), calls=%async_computation.4 | async-start | bytes 4194304 | tf_op jit(solution)/shard_map/all_to_all | solution.py:263
  639.3 143.1 %all-to-all-start.2 = ((bf16[1024,4,256]{0,2,1:T(8,128)(2,1)}), bf16[1024,4,256]{0,2,1:T(8,128)(2,1)}, u32[]{:S(2)}, u32[]{:S(2)}) async-start(bf16[1024,4,256]{0,2,1:T(8,128)(2,1)} %bitcast.180), calls=%async_computation.2 | async-start | bytes 4194304 | tf_op jit(solution)/shard_map/all_to_all | solution.py:226
  643.9 146.0 %collective-permute-start.1 = (bf16[3,656,256]{2,1,0:T(8,128)(2,1)}, bf16[3,656,256]{2,1,0:T(8,128)(2,1)}, u32[]{:S(2)}, u32[]{:S(2)}) collective-permute-start(bf16[3,656,256]{2,1,0:T(8,128)(2,1)} %bitcast.184), channel_id=1, source_target_pairs={{0,16},{16,0},{1,17},{17,1},{2,18},{18,2},{3,19},{19,3},{4,20},{20... | collective-permute-start | bytes 3022856 | tf_op jit(solution)/shard_map/ppermute | solution.py:175
  732.1 54.3 %copy-start.21 = (bf16[1,256,1024]{2,1,0:T(8,128)(2,1)S(1)}, bf16[1,256,1024]{2,1,0:T(8,128)(2,1)}, u32[]{:S(2)}) copy-start(bf16[1,256,1024]{2,1,0:T(8,128)(2,1)} %reduce-scatter.3.cloned.1.call-done) | copy-start | bytes 1572868
  732.1 54.3 %collective-permute-start = (bf16[256,1024]{1,0:T(8,128)(2,1)}, bf16[256,1024]{1,0:T(8,128)(2,1)}, u32[]{:S(2)}, u32[]{:S(2)}) collective-permute-start(bf16[256,1024]{1,0:T(8,128)(2,1)} %bitcast.186), channel_id=1, source_target_pairs={{0,16},{16,0},{1,17},{17,1},{2,18},{18,2},{3,19},{19,3},{4,20},{20... | collective-permute-start | bytes 1572872 | tf_op jit(solution)/shard_map/ppermute | solution.py:175
  782.4 7.5 copy-start.19
Sparse Core Ops, SparseCore 0:
  10.7 80.7 all-gather.4
  101.6 143.6 all-gather.6
  449.8 170.9 reduce-scatter.4
  624.7 107.3 reduce-scatter.2
